TPU v7x, 256 devices: a whole 4x4x8 slice. The times are simulated.
256 devices in a mesh: expert: 64 (over y, z, core), hidden: 4 (over x).
Axes of the slice: x: 4, y: 4, z: 8, core: 2. Of those that a mesh axis runs over, the one named last changes fastest.
Arguments:
- tokens: float32 [8192, 2048], P('expert', 'hidden'), may hold values from -6 to 6
- route_first: int32 [8192, 1], P('expert'), may hold values from 0 to 63; in each aligned block of 128 rows (0 to 127, 128 to 255, ...) at most 4 rows name the same one
- route_second: int32 [8192, 1], P('expert'), may hold values from 0 to 63; in each aligned block of 128 rows (0 to 127, 128 to 255, ...) at most 4 rows name the same one
- route_third: int32 [8192, 1], P('expert'), may hold values from 0 to 63; in each aligned block of 128 rows (0 to 127, 128 to 255, ...) at most 4 rows name the same one
- gate_weight: bfloat16 [64, 2048, 1024], P('expert', None, 'hidden'), may hold values from -0.125 to 0.125
- up_weight: bfloat16 [64, 2048, 1024], P('expert', None, 'hidden'), may hold values from -0.125 to 0.125
- down_weight: bfloat16 [64, 1024, 2048], P('expert', 'hidden'), may hold values from -0.1875 to 0.1875
- cotangent: float32 [8192, 2048], P('expert', 'hidden'), may hold values from -6 to 6
Outputs:
- grad_tokens: float32 [8192, 2048], P('expert', 'hidden')
- grad_gate: bfloat16 [64, 2048, 1024], P('expert', None, 'hidden')
- grad_up: bfloat16 [64, 2048, 1024], P('expert', None, 'hidden')
- grad_down: bfloat16 [64, 1024, 2048], P('expert', 'hidden')
Inputs may be any that keep to these rules, and one draw needn't show every extreme that they name: `route_first`: in the rows of one index of expert, no expert is named by more than 4 tokens in one visit, a bound that some block reaches; every expert is named somewhere. `route_second`: as for route_first. `route_third`: as for route_first.
All inputs are finite; a program needn't handle non-finite values.
Results may differ from a plain program's by a relative error of at most 0.024.
Values may be sent and summed in bfloat16 or wider, within the bound.
A program may use at most 64 MiB of HBM per device.

v0:
```python
import jax
import jax.numpy as jnp
from jax import lax
from jax.sharding import PartitionSpec as P


def from_everyone(value, axis):
    copies = jnp.broadcast_to(value, (lax.axis_size(axis), *value.shape))
    return lax.all_to_all(copies, axis, split_axis=0, concat_axis=0, tiled=True)


def joined_along(blocks, dim):
    blocks = jnp.moveaxis(blocks, 0, dim)
    shape = blocks.shape
    return blocks.reshape(*shape[:dim], shape[dim] * shape[dim + 1], *shape[dim + 2 :])


def gather_directly(value, axis, dim):
    blocks = from_everyone(value, axis)
    return joined_along(blocks, dim)


def cut_along(value, dim, count):
    shape = value.shape
    blocks = value.reshape(*shape[:dim], count, shape[dim] // count, *shape[dim + 1 :])
    return jnp.moveaxis(blocks, dim, 0)


def sent_and_summed(value, axis, dim):
    count = lax.axis_size(axis)
    blocks = lax.all_to_all(cut_along(value, dim, count), axis, 0, 0, tiled=True)
    return jnp.sum(blocks, axis=0)


def slot_table(route, experts, capacity):
    owner_ids = route[:, 0]
    onehot = (owner_ids[:, None] == jnp.arange(experts, dtype=jnp.int32)[None, :]).astype(jnp.int32)
    ranks = jnp.sum((jnp.cumsum(onehot, axis=0) - onehot) * onehot, axis=1)
    slots = owner_ids * capacity + ranks
    total = experts * capacity
    table = slots[None, :] == jnp.arange(total, dtype=jnp.int32)[:, None]
    return (slots, table)


def contract_first(left, right):
    return lax.dot_general(
        left, right, (((0,), (0,)), ((), ())), preferred_element_type=jnp.float32
    )


def contract_last(left, right):
    return lax.dot_general(
        left, right, (((1,), (1,)), ((), ())), preferred_element_type=jnp.float32
    )


def to_owner(rows, table, experts, capacity):
    placed = jnp.dot(table.astype(jnp.bfloat16), rows, preferred_element_type=jnp.float32).astype(
        jnp.bfloat16
    )
    placed = placed.reshape(experts, capacity, rows.shape[1])
    arrived = lax.all_to_all(placed, "expert", split_axis=0, concat_axis=0, tiled=True)
    arrived = arrived.reshape(experts * capacity, rows.shape[1])
    return gather_directly(arrived, "hidden", 1)


def send_home(partial_value, slots, experts, capacity):
    slot_rows, width = partial_value.shape
    shared = sent_and_summed(partial_value, "hidden", 1)
    back = lax.all_to_all(
        shared.reshape(experts, capacity, shared.shape[1]),
        "expert",
        split_axis=0,
        concat_axis=0,
        tiled=True,
    )
    back = back.reshape(slot_rows, shared.shape[1])
    return jnp.take(back, slots, axis=0)


def body(
    tokens, route_first, route_second, route_third, gate_weight, up_weight, down_weight, cotangent
):
    experts = lax.axis_size("expert")
    count = tokens.shape[0]
    capacity = 2 * count // experts
    gate_local = gate_weight[0]
    lift_local = up_weight[0]
    down_local = down_weight[0]
    routing = [
        slot_table(route, experts, capacity) for route in (route_first, route_second, route_third)
    ]
    state = tokens
    saved = []
    for visit in range(3):
        slots, table = routing[visit]
        inputs = to_owner(state.astype(jnp.bfloat16), table, experts, capacity)
        gate = jnp.dot(inputs, gate_local, preferred_element_type=jnp.float32)
        lifted = jnp.dot(inputs, lift_local, preferred_element_type=jnp.float32)
        saved.append((inputs, gate, lifted))
        if visit < 2:
            hidden = (jax.nn.sigmoid(gate) * gate * lifted).astype(jnp.bfloat16)
            partial_value = jnp.dot(hidden, down_local, preferred_element_type=jnp.float32)
            state = state + send_home(partial_value, slots, experts, capacity)
    grad = cotangent
    input_list = []
    hidden_list = []
    rows_list = []
    gate_list = []
    lift_list = []
    for visit in (2, 1, 0):
        slots, table = routing[visit]
        inputs, gate, lifted = saved[visit]
        grad_rows = to_owner(grad.astype(jnp.bfloat16), table, experts, capacity)
        sigma = jax.nn.sigmoid(gate)
        swish = gate * sigma
        hidden = (swish * lifted).astype(jnp.bfloat16)
        grad_hidden = contract_last(grad_rows, down_local)
        grad_gate = (grad_hidden * lifted * sigma * (1.0 + gate * (1.0 - sigma))).astype(
            jnp.bfloat16
        )
        grad_lift = (grad_hidden * swish).astype(jnp.bfloat16)
        input_list.append(inputs)
        hidden_list.append(hidden)
        rows_list.append(grad_rows)
        gate_list.append(grad_gate)
        lift_list.append(grad_lift)
        grad_inputs = contract_last(grad_gate, gate_local) + contract_last(grad_lift, lift_local)
        grad = grad + send_home(grad_inputs, slots, experts, capacity)
    all_inputs = jnp.concatenate(input_list, axis=0)
    total_down = contract_first(
        jnp.concatenate(hidden_list, axis=0), jnp.concatenate(rows_list, axis=0)
    )
    total_gate = contract_first(all_inputs, jnp.concatenate(gate_list, axis=0))
    total_lift = contract_first(all_inputs, jnp.concatenate(lift_list, axis=0))
    return (
        grad,
        total_gate.astype(jnp.bfloat16)[None],
        total_lift.astype(jnp.bfloat16)[None],
        total_down.astype(jnp.bfloat16)[None],
    )


def solution(mesh):
    placed = (
        P("expert", "hidden"),
        P("expert", None),
        P("expert", None),
        P("expert", None),
        P("expert", None, "hidden"),
        P("expert", None, "hidden"),
        P("expert", "hidden", None),
        P("expert", "hidden"),
    )
    return jax.shard_map(
        body,
        mesh=mesh,
        in_specs=placed,
        out_specs=(
            P("expert", "hidden"),
            P("expert", None, "hidden"),
            P("expert", None, "hidden"),
            P("expert", "hidden", None),
        ),
        check_vma=False,
    )
```

profile of v0, /device:TPU:1, one launch (start us, length us, event | category | flops | bytes accessed | tf_op | source)
XLA Modules:
  0.0 547.0 jit_solution(15255144909880064430)
XLA Ops:
  4.4 25.0 %all_to_all.110 = bf16[64,4,512]{2,1,0:T(4,128)(2,1)S(1)} all-to-all(bf16[64,4,512]{2,1,0:T(4,128)(2,1)S(1)} %reshape.137), channel_id=1, replica_groups=mesh['expert'=64,'hidden'=4] {'expert'}, dimensions={0} | all-to-all | bytes 524288 | tf_op jit(solution)/shard_map/all_to_all | solution.py:62
  30.6 4.4 all-to-all-start.3
  36.5 13.2 %all-to-all-done.3 = bf16[4,256,512]{1,2,0:T(8,128)(2,1)} async-done(((bf16[4,256,512]{1,2,0:T(8,128)(2,1)}), bf16[4,256,512]{1,2,0:T(8,128)(2,1)}, u32[]{:S(2)}, u32[]{:S(2)}) %all-to-all-start.3) | async-done | bytes 1048608 | tf_op jit(solution)/shard_map/all_to_all | solution.py:9
  54.4 27.9 %all_to_all.111 = f32[4,256,512]{2,1,0:T(8,128)} all-to-all(f32[4,256,512]{2,1,0:T(8,128)S(1)} %convolution_bitcast_fusion.1), channel_id=1, replica_groups=mesh['expert'=64,'hidden'=4] {'hidden'}, dimensions={0} | all-to-all | bytes 4194304 | tf_op jit(solution)/shard_map/all_to_all | solution.py:31
  85.1 8.3 %all-to-all-start.5 = ((f32[64,4,512]{2,1,0:T(4,128)}), f32[64,4,512]{2,1,0:T(4,128)}, u32[]{:S(2)}, u32[]{:S(2)}) async-start(f32[64,4,512]{2,1,0:T(4,128)} %reshape.140), calls=%async_computation.5 | async-start | bytes 1048576 | tf_op jit(solution)/shard_map/all_to_all | solution.py:70
  94.0 16.7 %all-to-all-done.5 = f32[64,4,512]{2,1,0:T(4,128)} async-done(((f32[64,4,512]{2,1,0:T(4,128)}), f32[64,4,512]{2,1,0:T(4,128)}, u32[]{:S(2)}, u32[]{:S(2)}) %all-to-all-start.5) | async-done | bytes 524320 | tf_op jit(solution)/shard_map/all_to_all | solution.py:70
  113.1 18.1 %all_to_all.112 = bf16[64,4,512]{2,1,0:T(4,128)(2,1)S(1)} all-to-all(bf16[64,4,512]{2,1,0:T(4,128)(2,1)S(1)} %reshape.142), channel_id=1, replica_groups=mesh['expert'=64,'hidden'=4] {'expert'}, dimensions={0} | all-to-all | bytes 524288 | tf_op jit(solution)/shard_map/all_to_all | solution.py:62
  131.4 17.2 %all_to_all.113 = bf16[4,256,512]{1,2,0:T(8,128)(2,1)S(1)} all-to-all(bf16[4,256,512]{1,2,0:T(8,128)(2,1)S(1)} %broadcast_in_dim.47), channel_id=1, replica_groups=mesh['expert'=64,'hidden'=4] {'hidden'}, dimensions={0} | all-to-all | bytes 2097152 | tf_op jit(solution)/shard_map/all_to_all | solution.py:9
  150.8 28.0 %all_to_all.114 = f32[4,256,512]{2,1,0:T(8,128)} all-to-all(f32[4,256,512]{2,1,0:T(8,128)S(1)} %convolution_bitcast_fusion), channel_id=1, replica_groups=mesh['expert'=64,'hidden'=4] {'hidden'}, dimensions={0} | all-to-all | bytes 4194304 | tf_op jit(solution)/shard_map/all_to_all | solution.py:31
  183.5 8.2 %all-to-all-start.9 = ((f32[64,4,512]{2,1,0:T(4,128)}), f32[64,4,512]{2,1,0:T(4,128)}, u32[]{:S(2)}, u32[]{:S(2)}) async-start(f32[64,4,512]{2,1,0:T(4,128)} %reshape.145), calls=%async_computation.9 | async-start | bytes 1048576 | tf_op jit(solution)/shard_map/all_to_all | solution.py:70
  193.8 15.2 %all-to-all-done.9 = f32[64,4,512]{2,1,0:T(4,128)} async-done(((f32[64,4,512]{2,1,0:T(4,128)}), f32[64,4,512]{2,1,0:T(4,128)}, u32[]{:S(2)}, u32[]{:S(2)}) %all-to-all-start.9) | async-done | bytes 524320 | tf_op jit(solution)/shard_map/all_to_all | solution.py:70
  209.0 6.5 %all-to-all-start = ((bf16[64,4,512]{2,1,0:T(4,128)(2,1)}), bf16[64,4,512]{2,1,0:T(4,128)(2,1)}, u32[]{:S(2)}, u32[]{:S(2)}) async-start(bf16[64,4,512]{2,1,0:T(4,128)(2,1)} %reshape.134), calls=%async_computation | async-start | bytes 524288 | tf_op jit(solution)/shard_map/all_to_all | solution.py:62
  219.2 8.2 %all-to-all-done = bf16[64,4,512]{2,1,0:T(4,128)(2,1)} async-done(((bf16[64,4,512]{2,1,0:T(4,128)(2,1)}), bf16[64,4,512]{2,1,0:T(4,128)(2,1)}, u32[]{:S(2)}, u32[]{:S(2)}) %all-to-all-start) | async-done | bytes 262176 | tf_op jit(solution)/shard_map/all_to_all | solution.py:62
  227.4 6.0 %all-to-all-start.10 = ((bf16[64,4,512]{2,1,0:T(4,128)(2,1)}), bf16[64,4,512]{2,1,0:T(4,128)(2,1)S(1)}, u32[]{:S(2)}, u32[]{:S(2)}) async-start(bf16[64,4,512]{2,1,0:T(4,128)(2,1)} %reshape.147), calls=%async_computation.10 | async-start | bytes 524288 | tf_op jit(solution)/shard_map/all_to_all | solution.py:62
  234.6 10.8 %all-to-all-done.10 = bf16[64,4,512]{2,1,0:T(4,128)(2,1)S(1)} async-done(((bf16[64,4,512]{2,1,0:T(4,128)(2,1)}), bf16[64,4,512]{2,1,0:T(4,128)(2,1)S(1)}, u32[]{:S(2)}, u32[]{:S(2)}) %all-to-all-start.10) | async-done | bytes 262176 | tf_op jit(solution)/shard_map/all_to_all | solution.py:62
  246.4 4.3 all-to-all-start.1
  252.7 12.9 %all-to-all-done.1 = bf16[4,256,512]{1,2,0:T(8,128)(2,1)} async-done(((bf16[4,256,512]{1,2,0:T(8,128)(2,1)}), bf16[4,256,512]{1,2,0:T(8,128)(2,1)}, u32[]{:S(2)}, u32[]{:S(2)}) %all-to-all-start.1) | async-done | bytes 1048608 | tf_op jit(solution)/shard_map/all_to_all | solution.py:9
  266.6 4.2 all-to-all-start.11
  272.5 12.2 %all-to-all-done.11 = bf16[4,256,512]{1,2,0:T(8,128)(2,1)} async-done(((bf16[4,256,512]{1,2,0:T(8,128)(2,1)}), bf16[4,256,512]{1,2,0:T(8,128)(2,1)}, u32[]{:S(2)}, u32[]{:S(2)}) %all-to-all-start.11) | async-done | bytes 1048608 | tf_op jit(solution)/shard_map/all_to_all | solution.py:9
  290.0 27.2 %all_to_all.115 = f32[4,256,512]{2,1,0:T(8,128)} all-to-all(f32[4,256,512]{2,1,0:T(8,128)S(1)} %bitcast.129), channel_id=1, replica_groups=mesh['expert'=64,'hidden'=4] {'hidden'}, dimensions={0} | all-to-all | bytes 4194304 | tf_op jit(solution)/shard_map/all_to_all | solution.py:31
  320.1 9.0 %all-to-all-start.13 = ((f32[64,4,512]{2,1,0:T(4,128)}), f32[64,4,512]{2,1,0:T(4,128)S(1)}, u32[]{:S(2)}, u32[]{:S(2)}) async-start(f32[64,4,512]{2,1,0:T(4,128)} %reshape.151), calls=%async_computation.13 | async-start | bytes 1048576 | tf_op jit(solution)/shard_map/all_to_all | solution.py:70
  329.1 17.3 %all-to-all-done.13 = f32[64,4,512]{2,1,0:T(4,128)S(1)} async-done(((f32[64,4,512]{2,1,0:T(4,128)}), f32[64,4,512]{2,1,0:T(4,128)S(1)}, u32[]{:S(2)}, u32[]{:S(2)}) %all-to-all-start.13) | async-done | bytes 524320 | tf_op jit(solution)/shard_map/all_to_all | solution.py:70
  348.4 18.1 %all_to_all.116 = bf16[64,4,512]{2,1,0:T(4,128)(2,1)S(1)} all-to-all(bf16[64,4,512]{2,1,0:T(4,128)(2,1)S(1)} %reshape.153), channel_id=1, replica_groups=mesh['expert'=64,'hidden'=4] {'expert'}, dimensions={0} | all-to-all | bytes 524288 | tf_op jit(solution)/shard_map/all_to_all | solution.py:62
  370.2 17.2 %all_to_all.117 = bf16[4,256,512]{1,2,0:T(8,128)(2,1)S(1)} all-to-all(bf16[4,256,512]{1,2,0:T(8,128)(2,1)S(1)} %broadcast_in_dim.49), channel_id=1, replica_groups=mesh['expert'=64,'hidden'=4] {'hidden'}, dimensions={0} | all-to-all | bytes 2097152 | tf_op jit(solution)/shard_map/all_to_all | solution.py:9
  389.7 28.0 %all_to_all.118 = f32[4,256,512]{2,1,0:T(8,128)} all-to-all(f32[4,256,512]{2,1,0:T(8,128)S(1)} %bitcast.130), channel_id=1, replica_groups=mesh['expert'=64,'hidden'=4] {'hidden'}, dimensions={0} | all-to-all | bytes 4194304 | tf_op jit(solution)/shard_map/all_to_all | solution.py:31
  419.8 25.4 %all_to_all.119 = f32[64,4,512]{2,1,0:T(4,128)} all-to-all(f32[64,4,512]{2,1,0:T(4,128)S(1)} %reshape.157), channel_id=1, replica_groups=mesh['expert'=64,'hidden'=4] {'expert'}, dimensions={0} | all-to-all | bytes 1048576 | tf_op jit(solution)/shard_map/all_to_all | solution.py:70
  449.9 18.1 %all_to_all.120 = bf16[64,4,512]{2,1,0:T(4,128)(2,1)S(1)} all-to-all(bf16[64,4,512]{2,1,0:T(4,128)(2,1)S(1)} %reshape.159), channel_id=1, replica_groups=mesh['expert'=64,'hidden'=4] {'expert'}, dimensions={0} | all-to-all | bytes 524288 | tf_op jit(solution)/shard_map/all_to_all | solution.py:62
  470.0 17.3 %all_to_all.121 = bf16[4,256,512]{1,2,0:T(8,128)(2,1)S(1)} all-to-all(bf16[4,256,512]{1,2,0:T(8,128)(2,1)S(1)} %broadcast_in_dim.50), channel_id=1, replica_groups=mesh['expert'=64,'hidden'=4] {'hidden'}, dimensions={0} | all-to-all | bytes 2097152 | tf_op jit(solution)/shard_map/all_to_all | solution.py:9
  489.5 27.2 %all_to_all.122 = f32[4,256,512]{2,1,0:T(8,128)S(1)} all-to-all(f32[4,256,512]{2,1,0:T(8,128)S(1)} %bitcast.131), channel_id=1, replica_groups=mesh['expert'=64,'hidden'=4] {'hidden'}, dimensions={0} | all-to-all | bytes 4194304 | tf_op jit(solution)/shard_map/all_to_all | solution.py:31
  519.9 8.0 %all-to-all-start.21 = ((f32[64,4,512]{2,1,0:T(4,128)}), f32[64,4,512]{2,1,0:T(4,128)S(1)}, u32[]{:S(2)}, u32[]{:S(2)}) async-start(f32[64,4,512]{2,1,0:T(4,128)} %reshape.163), calls=%async_computation.21 | async-start | bytes 1048576 | tf_op jit(solution)/shard_map/all_to_all | solution.py:70
  528.0 3.7 fusion.11
  538.8 6.5 %all-to-all-done.21 = f32[64,4,512]{2,1,0:T(4,128)S(1)} async-done(((f32[64,4,512]{2,1,0:T(4,128)}), f32[64,4,512]{2,1,0:T(4,128)S(1)}, u32[]{:S(2)}, u32[]{:S(2)}) %all-to-all-start.21) | async-done | bytes 524320 | tf_op jit(solution)/shard_map/all_to_all | solution.py:70
  (189 shorter events, 75.3 us)
Async XLA Ops:
  0.6 50.8 %copy-start = (bf16[1,2048,256]{2,1,0:T(8,128)(2,1)S(1)}, bf16[1,2048,256]{2,1,0:T(8,128)(2,1)}, u32[]{:S(2)}) copy-start(bf16[1,2048,256]{2,1,0:T(8,128)(2,1)} %param.15) | copy-start | bytes 3145732
  3.2 90.6 %copy-start.40 = (s32[128]{0:T(128)}, s32[128]{0:T(128)S(1)}, u32[]{:S(2)}) copy-start(s32[128]{0:T(128)S(1)} %get-tuple-element.10) | copy-start | bytes 1540
  30.6 19.1 %copy-start.1 = (bf16[1,2048,256]{2,1,0:T(8,128)(2,1)S(1)}, bf16[1,2048,256]{2,1,0:T(8,128)(2,1)}, u32[]{:S(2)}) copy-start(bf16[1,2048,256]{2,1,0:T(8,128)(2,1)} %param.14) | copy-start | bytes 3145732
  30.6 19.1 %all-to-all-start.3 = ((bf16[4,256,512]{1,2,0:T(8,128)(2,1)}), bf16[4,256,512]{1,2,0:T(8,128)(2,1)}, u32[]{:S(2)}, u32[]{:S(2)}) async-start(bf16[4,256,512]{1,2,0:T(8,128)(2,1)} %broadcast_in_dim.46), calls=%async_computation.3 | async-start | bytes 2097152 | tf_op jit(solution)/shard_map/all_to_all | solution.py:9
  36.5 17.5 %copy-start.2 = (bf16[2048,256]{1,0:T(8,128)(2,1)}, bf16[2048,256]{1,0:T(8,128)(2,1)S(1)}, u32[]{:S(2)}) copy-start(bf16[2048,256]{1,0:T(8,128)(2,1)S(1)} %copy.33) | copy-start | bytes 3145732
  85.1 25.6 %all-to-all-start.5 = ((f32[64,4,512]{2,1,0:T(4,128)}), f32[64,4,512]{2,1,0:T(4,128)}, u32[]{:S(2)}, u32[]{:S(2)}) async-start(f32[64,4,512]{2,1,0:T(4,128)} %reshape.140), calls=%async_computation.5 | async-start | bytes 1048576 | tf_op jit(solution)/shard_map/all_to_all | solution.py:70
  93.5 19.2 %copy-start.9 = (f32[128,512]{1,0:T(8,128)S(1)}, f32[128,512]{1,0:T(8,128)}, u32[]{:S(2)}) copy-start(f32[128,512]{1,0:T(8,128)} %param.10) | copy-start | bytes 786436
  94.0 19.0 %copy-start.41 = (s32[128]{0:T(128)}, s32[128]{0:T(128)S(1)}, u32[]{:S(2)}) copy-start(s32[128]{0:T(128)S(1)} %get-tuple-element.8) | copy-start | bytes 1540
  94.0 123.5 %copy-start.36 = (pred[128]{0:T(512)(128)(4,1)}, pred[128]{0:T(512)(128)(4,1)S(1)}, u32[]{:S(2)}) copy-start(pred[128]{0:T(512)(128)(4,1)S(1)} %get-tuple-element.7) | copy-start | bytes 388
  150.3 28.5 %copy-start.22 = (bf16[256,256]{1,0:T(8,128)(2,1)}, bf16[256,256]{1,0:T(8,128)(2,1)S(1)}, u32[]{:S(2)}) copy-start(bf16[256,256]{1,0:T(8,128)(2,1)S(1)} %get-tuple-element.20) | copy-start | bytes 393220
  178.8 12.9 %copy-start.39 = (s32[128,1]{0,1:T(1,128)S(1)}, s32[128,1]{0,1:T(1,128)}, u32[]{:S(2)}) copy-start(s32[128,1]{0,1:T(1,128)} %param.13) | copy-start | bytes 1540
  178.8 14.0 %copy-start.10 = (f32[128,512]{1,0:T(8,128)S(1)}, f32[128,512]{1,0:T(8,128)}, u32[]{:S(2)}) copy-start(f32[128,512]{1,0:T(8,128)} %param.17) | copy-start | bytes 786436
  181.5 33.9 %copy-start.42 = (s32[128]{0:T(128)S(1)}, s32[128]{0:T(128)}, u32[]{:S(2)}) copy-start(s32[128]{0:T(128)} %copy-done.41) | copy-start | bytes 1540
  183.5 25.5 %all-to-all-start.9 = ((f32[64,4,512]{2,1,0:T(4,128)}), f32[64,4,512]{2,1,0:T(4,128)}, u32[]{:S(2)}, u32[]{:S(2)}) async-start(f32[64,4,512]{2,1,0:T(4,128)} %reshape.145), calls=%async_computation.9 | async-start | bytes 1048576 | tf_op jit(solution)/shard_map/all_to_all | solution.py:70
  192.8 22.7 %copy-start.43 = (s32[128]{0:T(128)}, s32[128]{0:T(128)S(1)}, u32[]{:S(2)}) copy-start(s32[128]{0:T(128)S(1)} %get-tuple-element.6) | copy-start | bytes 1540
  209.0 18.4 %all-to-all-start = ((bf16[64,4,512]{2,1,0:T(4,128)(2,1)}), bf16[64,4,512]{2,1,0:T(4,128)(2,1)}, u32[]{:S(2)}, u32[]{:S(2)}) async-start(bf16[64,4,512]{2,1,0:T(4,128)(2,1)} %reshape.134), calls=%async_computation | async-start | bytes 524288 | tf_op jit(solution)/shard_map/all_to_all | solution.py:62
  227.4 18.0 %all-to-all-start.10 = ((bf16[64,4,512]{2,1,0:T(4,128)(2,1)}), bf16[64,4,512]{2,1,0:T(4,128)(2,1)S(1)}, u32[]{:S(2)}, u32[]{:S(2)}) async-start(bf16[64,4,512]{2,1,0:T(4,128)(2,1)} %reshape.147), calls=%async_computation.10 | async-start | bytes 524288 | tf_op jit(solution)/shard_map/all_to_all | solution.py:62
  246.4 19.1 %all-to-all-start.1 = ((bf16[4,256,512]{1,2,0:T(8,128)(2,1)}), bf16[4,256,512]{1,2,0:T(8,128)(2,1)}, u32[]{:S(2)}, u32[]{:S(2)}) async-start(bf16[4,256,512]{1,2,0:T(8,128)(2,1)} %broadcast_in_dim.45), calls=%async_computation.1 | async-start | bytes 2097152 | tf_op jit(solution)/shard_map/all_to_all | solution.py:9
  251.5 19.3 %copy-start.4 = (bf16[1,256,2048]{2,1,0:T(8,128)(2,1)S(1)}, bf16[1,256,2048]{2,1,0:T(8,128)(2,1)}, u32[]{:S(2)}) copy-start(bf16[1,256,2048]{2,1,0:T(8,128)(2,1)} %param.16) | copy-start | bytes 3145732
  266.6 18.2 %all-to-all-start.11 = ((bf16[4,256,512]{1,2,0:T(8,128)(2,1)}), bf16[4,256,512]{1,2,0:T(8,128)(2,1)}, u32[]{:S(2)}, u32[]{:S(2)}) async-start(bf16[4,256,512]{1,2,0:T(8,128)(2,1)} %broadcast_in_dim.48), calls=%async_computation.11 | async-start | bytes 2097152 | tf_op jit(solution)/shard_map/all_to_all | solution.py:9
  320.1 27.3 %copy-start.11 = (f32[128,512]{1,0:T(8,128)S(1)}, f32[128,512]{1,0:T(8,128)}, u32[]{:S(2)}) copy-start(f32[128,512]{1,0:T(8,128)} %param.17) | copy-start | bytes 786436
  320.1 26.3 %all-to-all-start.13 = ((f32[64,4,512]{2,1,0:T(4,128)}), f32[64,4,512]{2,1,0:T(4,128)S(1)}, u32[]{:S(2)}, u32[]{:S(2)}) async-start(f32[64,4,512]{2,1,0:T(4,128)} %reshape.151), calls=%async_computation.13 | async-start | bytes 1048576 | tf_op jit(solution)/shard_map/all_to_all | solution.py:70
  367.3 20.2 %copy-start.5 = (bf16[1,256,2048]{2,1,0:T(8,128)(2,1)S(1)}, bf16[1,256,2048]{2,1,0:T(8,128)(2,1)}, u32[]{:S(2)}) copy-start(bf16[1,256,2048]{2,1,0:T(8,128)(2,1)} %param.16) | copy-start | bytes 3145732
  369.1 18.3 %copy-start.21 = (f32[256,256]{1,0:T(8,128)S(1)}, f32[256,256]{1,0:T(8,128)}, u32[]{:S(2)}) copy-start(f32[256,256]{1,0:T(8,128)} %copy-done.20) | copy-start | bytes 786436
  369.1 18.3 %copy-start.46 = (f32[256,256]{1,0:T(8,128)S(1)}, f32[256,256]{1,0:T(8,128)}, u32[]{:S(2)}) copy-start(f32[256,256]{1,0:T(8,128)} %get-tuple-element.21) | copy-start | bytes 786436
  419.8 28.1 %copy-start.12 = (f32[128,512]{1,0:T(8,128)S(1)}, f32[128,512]{1,0:T(8,128)}, u32[]{:S(2)}) copy-start(f32[128,512]{1,0:T(8,128)} %param.17) | copy-start | bytes 786436
  419.8 28.1 %copy-start.37 = (pred[128]{0:T(512)(128)(4,1)S(1)}, pred[128]{0:T(512)(128)(4,1)}, u32[]{:S(2)}) copy-start(pred[128]{0:T(512)(128)(4,1)} %copy-done.36) | copy-start | bytes 388
  448.9 19.0 %copy-start.13 = (f32[128,512]{1,0:T(8,128)}, f32[128,512]{1,0:T(8,128)S(1)}, u32[]{:S(2)}) copy-start(f32[128,512]{1,0:T(8,128)S(1)} %select_add_fusion.1) | copy-start | bytes 786436
  468.7 18.6 %copy-start.6 = (bf16[1,256,2048]{2,1,0:T(8,128)(2,1)S(1)}, bf16[1,256,2048]{2,1,0:T(8,128)(2,1)}, u32[]{:S(2)}) copy-start(bf16[1,256,2048]{2,1,0:T(8,128)(2,1)} %param.16) | copy-start | bytes 3145732
  469.9 17.4 %copy-start.19 = (f32[256,256]{1,0:T(8,128)S(1)}, f32[256,256]{1,0:T(8,128)}, u32[]{:S(2)}) copy-start(f32[256,256]{1,0:T(8,128)} %copy-done.18) | copy-start | bytes 786436
  469.9 17.4 %copy-start.45 = (f32[256,256]{1,0:T(8,128)S(1)}, f32[256,256]{1,0:T(8,128)}, u32[]{:S(2)}) copy-start(f32[256,256]{1,0:T(8,128)} %get-tuple-element.19) | copy-start | bytes 786436
  519.9 25.4 %all-to-all-start.21 = ((f32[64,4,512]{2,1,0:T(4,128)}), f32[64,4,512]{2,1,0:T(4,128)S(1)}, u32[]{:S(2)}, u32[]{:S(2)}) async-start(f32[64,4,512]{2,1,0:T(4,128)} %reshape.163), calls=%async_computation.21 | async-start | bytes 1048576 | tf_op jit(solution)/shard_map/all_to_all | solution.py:70
  (25 other events, 101.5 us)
where the time goes:
time: 549 us; the launch traced here: 547 us
  blocking collectives  295 us (54%)
  waiting for transfers between devices  113 us (21%)
  starting transfers between devices  59 us (11%)
  local copies, waits for them, and re-layouts  32.2 us (6%)
  matrix products  31.5 us (6%)
  other arithmetic  15.2 us (3%)
    all_to_all x5, blocking collectives, sent_and_summed(): lax.all_to_all(cut_along(value, dim, count), axis, 0, 0, tiled=True)  138 us
    all_to_all x4, blocking collectives, to_owner(): lax.all_to_all(placed, 'expert', split_axis=0, concat_axis=0, tiled=True)  79.2 us
    all_to_all x4, waiting for transfers between devices, send_home(): lax.all_to_all(shared.reshape(experts, capacity, shared.shape[1]), 'exper...  55.7 us
    all_to_all x3, blocking collectives, from_everyone(): return lax.all_to_all(copies, axis, split_axis=0, concat_axis=0, tiled=True)  51.7 us
    all_to_all x3, waiting for transfers between devices, from_everyone(): return lax.all_to_all(copies, axis, split_axis=0, concat_axis=0, tiled=True)  38.3 us
    all_to_all x4, starting transfers between devices, send_home(): lax.all_to_all(shared.reshape(experts, capacity, shared.shape[1]), 'exper...  33.6 us
    all_to_all x1, blocking collectives, send_home(): lax.all_to_all(shared.reshape(experts, capacity, shared.shape[1]), 'exper...  25.4 us
    all_to_all x2, waiting for transfers between devices, to_owner(): lax.all_to_all(placed, 'expert', split_axis=0, concat_axis=0, tiled=True)  19 us
  transfers between devices with their start and end apart: 9, of which 9 were waited for; matrix products, arithmetic and copies ran while one was open for 4% of the time, Pallas kernels for 0%

commit v1 on v0

v1 whole, which is shorter than its diff:
```python
import jax
import jax.numpy as jnp
from jax import lax
from jax.experimental import pallas as pl
from jax.experimental.pallas import tpu as pltpu
from jax.sharding import PartitionSpec as P

MESH = pl.DeviceIdType.MESH
F32 = jnp.float32
BF16 = jnp.bfloat16
EXPERTS = 64
RANKS = 4
HIDDEN = 4
VMEM = pltpu.VMEM


def dot(a, b):
    return jnp.dot(a, b, preferred_element_type=F32)


def contract_last(a, b):
    return lax.dot_general(a, b, (((1,), (1,)), ((), ())), preferred_element_type=F32)


def contract_first(a, b):
    return lax.dot_general(a, b, (((0,), (0,)), ((), ())), preferred_element_type=F32)


def exact_ones(condition):
    return jnp.where(condition, 1.0, 0.0).astype(BF16)


def kernel(
    tok, cot, krow, kcol, gate_hbm, up_hbm, down_hbm,
    out_tok, out_gate, out_up, out_down,
    wg, wu, wd, place, fetch, perm, perm_t, sent, got, rows_of, part_out, relayed, summed,
    gate, lift, hid, dgate, dup, own, acc_gate, acc_up, acc_down, res_gate, res_up, res_down, state, grad,
    sem_w, sem_send, sem_got, sem_xs, sem_xr, sem_ys, sem_yr,
):
    me = lax.axis_index("expert")
    h = lax.axis_index("hidden")
    right, left, across = lax.rem(h + 1, HIDDEN), lax.rem(h + 3, HIDDEN), lax.rem(h + 2, HIDDEN)

    loads = [
        pltpu.make_async_copy(gate_hbm, wg, sem_w.at[0]),
        pltpu.make_async_copy(up_hbm, wu, sem_w.at[1]),
    ] + [
        pltpu.make_async_copy(down_hbm.at[:, pl.ds(k * 512, 512)], wd.at[k], sem_w.at[2 + k])
        for k in range(HIDDEN)
    ]
    for load in loads:
        load.start()

    barrier = pltpu.get_barrier_semaphore()

    def greet(j, carry):
        pl.semaphore_signal(barrier, inc=1, device_id=(lax.rem(me + j, EXPERTS), h), device_id_type=MESH)
        return carry

    lax.fori_loop(1, EXPERTS, greet, 0)
    for side in (left, right):
        pl.semaphore_signal(barrier, inc=1, device_id=(me, side), device_id_type=MESH)

    def build(visit):
        def step(g, carry):
            rows = pl.ds(pl.multiple_of(g * 256, 256), 256)
            numbers = lax.broadcasted_iota(jnp.int32, (256, 512), 0) + g * 256
            place[visit, rows, :] = exact_ones(numbers == krow[visit])
            half = pl.ds(pl.multiple_of(g * 128, 128), 128)
            across_lanes = lax.broadcasted_iota(jnp.int32, (128, 1024), 1)
            fetch[visit, half, :] = exact_ones(across_lanes == kcol[visit, half, :])
            return carry

        lax.fori_loop(0, 4, step, 0)

    def image(slot_number):
        c, s = slot_number // 64, slot_number % 64
        return (s // 4) * 16 + c * 4 + s % 4

    first = lax.broadcasted_iota(jnp.int32, (256, 256), 0)
    second = lax.broadcasted_iota(jnp.int32, (256, 256), 1)
    perm[...] = exact_ones(second == image(first))
    perm_t[...] = exact_ones(first == image(second))
    build(0)
    state[...] = tok[...]
    grad[...] = cot[...]
    pl.semaphore_wait(barrier, EXPERTS + 1)

    pending = []

    def send_group(n, g, forward):
        def go(j, carry):
            rows = pl.ds(pl.multiple_of(j * 16, 16), 16)
            step = j if forward else EXPERTS - j
            pltpu.make_async_remote_copy(
                src_ref=sent.at[n, rows], dst_ref=got.at[n, rows],
                send_sem=sem_send.at[n], recv_sem=sem_got.at[n],
                device_id=(lax.rem(me + step, EXPERTS), h), device_id_type=MESH,
            ).start()
            return carry

        lax.fori_loop(max(1, g * 16), g * 16 + 16, go, 0)

    def whole(n):
        rows = pl.ds(16, (EXPERTS - 1) * 16)
        return pltpu.make_async_remote_copy(
            src_ref=sent.at[n, rows], dst_ref=got.at[n, rows],
            send_sem=sem_send.at[n], recv_sem=sem_got.at[n],
            device_id=(lax.rem(me + 1, EXPERTS), h), device_id_type=MESH,
        )

    def exchanged(n):
        whole(n).wait_recv()
        pending.append(whole(n))

    def dispatch(n, visit, values):
        values = values.astype(BF16)
        stacked = jnp.concatenate([values[:, c * 128 : (c + 1) * 128] for c in range(4)], axis=0)
        for g in range(4):
            rows = pl.ds(g * 256, 256)
            sent[n, rows, :] = dot(place[visit, rows, :], stacked).astype(BF16)
            send_group(n, g, True)
        got[n, 0:16, :] = sent[n, 0:16, :]

    def hand(ref_from, ref_to, s, r, side):
        copy = pltpu.make_async_remote_copy(
            src_ref=ref_from, dst_ref=ref_to, send_sem=s, recv_sem=r,
            device_id=(me, side), device_id_type=MESH,
        )
        copy.start()
        pending.append(copy)

    def awaited(ref, s, r):
        pltpu.make_async_remote_copy(
            src_ref=ref, dst_ref=ref, send_sem=s, recv_sem=r, device_id=(me, right), device_id_type=MESH
        ).wait_recv()

    def spread(n, d):
        exchanged(n)
        for g in range(4):
            turned = dot(perm[...], got[n, pl.ds(g * 256, 256), :]).astype(BF16)
            rows = pl.ds(g * 64, 64)
            for c in range(4):
                rows_of[d, h, rows, pl.ds(c * 128, 128)] = turned[c * 64 : (c + 1) * 64]
            mine = rows_of.at[d, h, rows]
            hand(mine, mine, sem_xs.at[d, 0, g], sem_xr.at[d, 0, g], right)
            hand(mine, mine, sem_xs.at[d, 1, g], sem_xr.at[d, 1, g], left)

    def relay(d):
        for g in range(4):
            rows = pl.ds(g * 64, 64)
            from_left, from_right = rows_of.at[d, left, rows], rows_of.at[d, right, rows]
            awaited(from_left, sem_xs.at[d, 0, g], sem_xr.at[d, 0, g])
            if g % 2 == 0:
                hand(from_left, from_left, sem_xs.at[d, 2, g], sem_xr.at[d, 2, g], right)
            awaited(from_right, sem_xs.at[d, 1, g], sem_xr.at[d, 1, g])
            if g % 2 == 1:
                hand(from_right, from_right, sem_xs.at[d, 2, g], sem_xr.at[d, 2, g], left)

    def last_quarter(d):
        for g in range(4):
            awaited(rows_of.at[d, across, pl.ds(g * 64, 64)], sem_xs.at[d, 2, g], sem_xr.at[d, 2, g])

    def gathered(d, use):
        use(h, True)
        relay(d)
        use(left, False)
        use(right, False)
        last_quarter(d)
        use(across, False)

    def go_home(n, d, part):
        upper, lower = pl.ds(0, 128), pl.ds(128, 128)
        for half, side, slot in ((0, right, 0), (1, left, 1)):
            rows = pl.ds(half * 128, 128)
            part_out[d, 0, rows, :] = part(across, half).astype(BF16)
            hand(part_out.at[d, 0, rows], relayed.at[d, slot], sem_ys.at[d, slot], sem_yr.at[d, slot], side)
        part_out[d, 1, lower, :] = part(right, 1).astype(BF16)
        hand(part_out.at[d, 1, lower], summed.at[d, 0, lower], sem_ys.at[d, 2], sem_yr.at[d, 2], right)
        part_out[d, 2, upper, :] = part(left, 0).astype(BF16)
        hand(part_out.at[d, 2, upper], summed.at[d, 1, upper], sem_ys.at[d, 3], sem_yr.at[d, 3], left)
        ahead = part(right, 0)
        awaited(relayed.at[d, 0], sem_ys.at[d, 0], sem_yr.at[d, 0])
        part_out[d, 1, upper, :] = (ahead + relayed[d, 0].astype(F32)).astype(BF16)
        hand(part_out.at[d, 1, upper], summed.at[d, 0, upper], sem_ys.at[d, 4], sem_yr.at[d, 4], right)
        behind = part(left, 1)
        awaited(relayed.at[d, 1], sem_ys.at[d, 1], sem_yr.at[d, 1])
        part_out[d, 2, lower, :] = (behind + relayed[d, 1].astype(F32)).astype(BF16)
        hand(part_out.at[d, 2, lower], summed.at[d, 1, lower], sem_ys.at[d, 5], sem_yr.at[d, 5], left)
        for half in range(2):
            own[pl.ds(half * 128, 128), :] = part(h, half)
        for half in range(2):
            rows = pl.ds(half * 128, 128)
            a, b = (4, 3) if half == 0 else (2, 5)
            awaited(summed.at[d, 0, rows], sem_ys.at[d, a], sem_yr.at[d, a])
            awaited(summed.at[d, 1, rows], sem_ys.at[d, b], sem_yr.at[d, b])
            total = own[rows, :] + summed[d, 0, rows, :].astype(F32) + summed[d, 1, rows, :].astype(F32)
            total = total.astype(BF16)
            for g in (2 * half, 2 * half + 1):
                piece = total[(g % 2) * 64 : (g % 2) * 64 + 64]
                stacked = jnp.concatenate([piece[:, c * 128 : (c + 1) * 128] for c in range(4)], axis=0)
                sent[n, pl.ds(g * 256, 256), :] = dot(perm_t[...], stacked).astype(BF16)
                send_group(n, g, False)
        got[n, 0:16, :] = sent[n, 0:16, :]

    def arrive(n, visit, target):
        exchanged(n)
        back = dot(fetch[visit], got[n])
        for c in range(4):
            target[:, pl.ds(c * 128, 128)] += back[c * 128 : (c + 1) * 128]

    def lift_up(visit):
        def use(k, start):
            a = rows_of[visit, k]
            if start:
                gate[visit] = dot(a, wg[k])
                lift[visit] = dot(a, wu[k])
            else:
                gate[visit] += dot(a, wg[k])
                lift[visit] += dot(a, wu[k])

        gathered(visit, use)
        z = gate[visit]
        hid[visit] = (jax.nn.sigmoid(z) * z * lift[visit]).astype(BF16)

    def put_down(visit):
        def part(k, half):
            return dot(hid[visit, pl.ds(half * 128, 128), :], wd[k])

        return part

    def put_back(k, half):
        rows = pl.ds(half * 128, 128)
        return contract_last(dgate[rows, :], wg[k]) + contract_last(dup[rows, :], wu[k])

    def turn(d, visit):
        def use(k, start):
            value = contract_last(rows_of[d, k], wd[k])
            if start:
                own[:, 0:256] = value
            else:
                own[:, 0:256] += value

        gathered(d, use)
        q, z = own[:, 0:256], gate[visit]
        sigma = jax.nn.sigmoid(z)
        dgate[...] = (q * lift[visit] * sigma * (1.0 + z * (1.0 - sigma))).astype(BF16)
        dup[...] = (q * (z * sigma)).astype(BF16)

    def weigh(d, visit):
        def step(k, carry):
            a, b = rows_of[visit, k], rows_of[d, k]
            by_gate = contract_first(a, dgate[...])
            by_up = contract_first(a, dup[...])
            by_down = contract_first(hid[visit], b)
            if visit < 2:
                by_gate += acc_gate[k]
                by_up += acc_up[k]
                by_down += acc_down[k]
            if visit > 0:
                acc_gate[k] = by_gate
                acc_up[k] = by_up
                acc_down[k] = by_down
            else:
                res_gate[k] = by_gate.astype(BF16)
                res_up[k] = by_up.astype(BF16)
                res_down[k] = by_down.astype(BF16)
            return carry

        lax.fori_loop(0, HIDDEN, step, 0)

    dispatch(0, 0, state[...])
    for load in loads:
        load.wait()
    build(2)
    spread(0, 0)
    dispatch(1, 2, grad[...])
    lift_up(0)
    go_home(2, 0, put_down(0))
    build(1)
    spread(1, 3)
    relay(3)
    arrive(2, 0, state)

    dispatch(3, 1, state[...])
    last_quarter(3)
    spread(3, 1)
    lift_up(1)
    go_home(4, 1, put_down(1))
    arrive(4, 1, state)

    dispatch(5, 2, state[...])
    for k in range(HIDDEN):
        value = contract_last(rows_of[3, k], wd[k])
        if k == 0:
            own[:, 0:256] = value
        else:
            own[:, 0:256] += value
    spread(5, 2)
    lift_up(2)
    q, z = own[:, 0:256], gate[2]
    sigma = jax.nn.sigmoid(z)
    dgate[...] = (q * lift[2] * sigma * (1.0 + z * (1.0 - sigma))).astype(BF16)
    dup[...] = (q * (z * sigma)).astype(BF16)
    go_home(6, 2, put_back)
    weigh(3, 2)
    arrive(6, 2, grad)

    dispatch(7, 1, grad[...])
    spread(7, 4)
    turn(4, 1)
    go_home(8, 3, put_back)
    weigh(4, 1)
    arrive(8, 1, grad)

    dispatch(9, 0, grad[...])
    spread(9, 5)
    turn(5, 0)
    go_home(10, 4, put_back)
    weigh(5, 0)
    stores = [
        pltpu.make_async_copy(res_gate, out_gate, sem_w.at[0]),
        pltpu.make_async_copy(res_up, out_up, sem_w.at[1]),
    ] + [
        pltpu.make_async_copy(res_down.at[k], out_down.at[:, pl.ds(k * 512, 512)], sem_w.at[2 + k])
        for k in range(HIDDEN)
    ]
    for store in stores:
        store.start()
    arrive(10, 0, grad)
    out_tok[...] = grad[...]
    for copy in pending:
        copy.wait_send()
    for store in stores:
        store.wait()


def body(
    tokens, route_first, route_second, route_third, gate_weight, up_weight, down_weight, cotangent
):
    count, width = tokens.shape
    me = lax.axis_index("expert")
    owner = jnp.stack([route[:, 0] for route in (route_first, route_second, route_third)])
    earlier = jnp.arange(count)[None, :] < jnp.arange(count)[:, None]
    same = (owner[:, :, None] == owner[:, None, :]) & earlier[None]
    rank = jnp.sum(same.astype(jnp.int32), axis=2)
    base = lax.rem(owner - me + EXPERTS, EXPERTS) * (4 * RANKS) + rank
    keys = base[:, None, :] + RANKS * jnp.arange(4, dtype=jnp.int32)[None, :, None]
    keys = keys.reshape(3, 4 * count)

    in_vmem = pl.BlockSpec(memory_space=VMEM)
    anywhere = pl.BlockSpec(memory_space=pl.ANY)
    dma = pltpu.SemaphoreType.DMA
    out_tok, out_gate, out_up, out_down = pl.pallas_call(
        kernel,
        out_shape=(
            jax.ShapeDtypeStruct((count, width), F32),
            jax.ShapeDtypeStruct((4, 512, 256), BF16),
            jax.ShapeDtypeStruct((4, 512, 256), BF16),
            jax.ShapeDtypeStruct((256, 2048), BF16),
        ),
        in_specs=[in_vmem] * 4 + [anywhere] * 3,
        out_specs=(in_vmem, anywhere, anywhere, anywhere),
        scratch_shapes=[
            VMEM((4, 512, 256), BF16),
            VMEM((4, 512, 256), BF16),
            VMEM((4, 256, 512), BF16),
            VMEM((3, 1024, 512), BF16),
            VMEM((3, 512, 1024), BF16),
            VMEM((256, 256), BF16),
            VMEM((256, 256), BF16),
            VMEM((11, 1024, 128), BF16),
            VMEM((11, 1024, 128), BF16),
            VMEM((6, 4, 256, 512), BF16),
            VMEM((5, 3, 256, 512), BF16),
            VMEM((5, 2, 128, 512), BF16),
            VMEM((5, 2, 256, 512), BF16),
            VMEM((3, 256, 256), F32),
            VMEM((3, 256, 256), F32),
            VMEM((3, 256, 256), BF16),
            VMEM((256, 256), BF16),
            VMEM((256, 256), BF16),
            VMEM((256, 512), F32),
            VMEM((4, 512, 256), F32),
            VMEM((4, 512, 256), F32),
            VMEM((4, 256, 512), F32),
            VMEM((4, 512, 256), BF16),
            VMEM((4, 512, 256), BF16),
            VMEM((4, 256, 512), BF16),
            VMEM((128, 512), F32),
            VMEM((128, 512), F32),
            dma((6,)),
            dma((11,)),
            dma((11,)),
            dma((6, 3, 4)),
            dma((6, 3, 4)),
            dma((5, 6)),
            dma((5, 6)),
        ],
        compiler_params=pltpu.CompilerParams(
            collective_id=0, has_side_effects=True, vmem_limit_bytes=58 * 2**20
        ),
    )(
        tokens,
        cotangent,
        keys[:, None, :],
        keys[:, :, None],
        gate_weight.reshape(4, 512, 256),
        up_weight.reshape(4, 512, 256),
        down_weight[0],
    )
    return (
        out_tok,
        out_gate.reshape(1, 2048, 256),
        out_up.reshape(1, 2048, 256),
        out_down[None],
    )


def solution(mesh):
    placed = (
        P("expert", "hidden"),
        P("expert", None),
        P("expert", None),
        P("expert", None),
        P("expert", None, "hidden"),
        P("expert", None, "hidden"),
        P("expert", "hidden", None),
        P("expert", "hidden"),
    )
    return jax.shard_map(
        body,
        mesh=mesh,
        in_specs=placed,
        out_specs=(
            P("expert", "hidden"),
            P("expert", None, "hidden"),
            P("expert", None, "hidden"),
            P("expert", "hidden", None),
        ),
        check_vma=False,
    )
```

time: 549 us -> 235 us (0.43)
  blocking collectives: 295 us -> 0 us
  Pallas kernels: 0 us -> 224 us
  waiting for transfers between devices: 113 us -> 0 us
  starting transfers between devices: 59 us -> 0 us
  matrix products: 31.5 us -> 0 us
  local copies, waits for them, and re-layouts: 32.2 us -> 7.89 us
  other arithmetic: 15.2 us -> 1.89 us
    all_to_all x13 -> x0, blocking collectives: 295 us -> none  [the longest x5 138 us: sent_and_summed(): lax.all_to_all(cut_along(value, dim, count), axis, 0, 0, tiled=True)]
    pallas_call x0 -> x1, Pallas kernels: none -> 224 us  [body(): pl.pallas_call(kernel, out_shape=(jax.ShapeDtypeStruct((count, width), F3...]
    all_to_all x9 -> x0, waiting for transfers between devices: 113 us -> none  [the longest x4 55.7 us: send_home(): lax.all_to_all(shared.reshape(experts, capacity, shared.shape[1]), 'exper...]
    all_to_all x9 -> x0, starting transfers between devices: 59 us -> none  [the longest x4 33.6 us: send_home(): lax.all_to_all(shared.reshape(experts, capacity, shared.shape[1]), 'exper...]
    dot_general x26 -> x0, matrix products: 31.5 us -> none  [the longest x3 10.7 us: contract_first(): lax.dot_general(left, right, (((0,), (0,)), ((), ())), preferred_element_...]
    reshape x31 -> x0, local copies, waits for them, and re-layouts: 20.6 us -> none  [the longest x12 8.06 us: to_owner(): arrived = arrived.reshape(experts * capacity, rows.shape[1])]
    reduce_sum x8 -> x1, other arithmetic: 10.5 us -> 0.23 us  [body(): rank = jnp.sum(same.astype(jnp.int32), axis=2)]
    unnamed x96 -> x14, local copies, waits for them, and re-layouts: 1.31 us -> 7.19 us
  transfers between devices with their start and end apart: 9 -> 0, of which waited for: 9 -> 0; matrix products, arithmetic and copies ran while one was open for 4% -> 0% of each run, Pallas kernels for 0% -> 0%
where the time goes in v1:
time: 235 us
  Pallas kernels  224 us (95%)
  local copies, waits for them, and re-layouts  7.89 us (3%)
    pallas_call x1, Pallas kernels, body(): pl.pallas_call(kernel, out_shape=(jax.ShapeDtypeStruct((count, width), F3...  224 us
    unnamed x14, local copies, waits for them, and re-layouts  7.19 us

profile of v1, /device:TPU:1, one launch (start us, length us, event | category | flops | bytes accessed | tf_op | source)
XLA Modules:
  0.0 234.5 jit_solution(7326367883052234301)
XLA Ops:
  0.6 0.0 copy-start.2
  0.7 0.0 copy-start.3
  0.7 0.0 copy-start.4
  0.7 0.1 broadcast_bitcast_fusion
  0.8 0.6 copy-done.2
  1.3 0.0 copy-done.3
  1.3 0.0 copy-done.4
  1.4 0.2 convert_reduce_fusion
  1.6 0.6 broadcast_add_fusion.1.krow
  2.2 0.6 add.68
  2.9 1.0 broadcast_add_fusion.kcol
  3.9 224.1 %shard_map.111 = (f32[128,512]{1,0:T(8,128)}, bf16[4,512,256]{2,1,0:T(8,128)(2,1)}, bf16[4,512,256]{2,1,0:T(8,128)(2,1)}, bf16[256,2048]{1,0:T(8,128)(2,1)}) custom-call(f32[128,512]{1,0:T(8,128)} %tok.1, f32[128,512]{1,0:T(8,128)} %cot.1, s32[3,1,512]{2,1,0:T(1,128)} %broadcast_add_fusion.1.krow, s32[3,512,1]{2,1,0:T(8,128)} %broadcast_add_fusion.kcol, ...), custom_call_target="tpu_custom_call" | custom-call | tf_op jit(solution)/shard_map/pallas_call | solution.py:354
  227.9 1.7 copy.20
  229.6 0.0 copy-start.1
  229.6 2.4 %copy.21 = bf16[1,2048,256]{2,1,0:T(8,128)(2,1)} copy(bf16[1,2048,256]{2,1,0:T(8,128)(2,1)} %bitcast.17) | data formatting | bytes 2097152
  232.0 0.0 copy-done.1
  232.0 0.0 copy-start
  232.0 1.0 copy.22
  232.9 0.6 copy-done
  233.6 1.0 copy.23
  (5 shorter events, 0.1 us)
Async XLA Ops:
  0.6 0.7 copy-start.2
  0.7 0.7 copy-start.3
  0.7 0.7 copy-start.4
  229.6 2.4 %copy-start.1 = (bf16[4,512,256]{2,1,0:T(8,128)(2,1)S(1)}, bf16[4,512,256]{2,1,0:T(8,128)(2,1)}, u32[]{:S(2)}) copy-start(bf16[4,512,256]{2,1,0:T(8,128)(2,1)} %get-tuple-element.10) | copy-start | bytes 3145732
  232.0 1.6 copy-start

commit v2 on v1

v2 whole, which is shorter than its diff:
```python
import jax
import jax.numpy as jnp
from jax import lax
from jax.experimental import pallas as pl
from jax.experimental.pallas import tpu as pltpu
from jax.sharding import PartitionSpec as P

MESH = pl.DeviceIdType.MESH
F32 = jnp.float32
BF16 = jnp.bfloat16
EXPERTS = 64
RANKS = 4
HIDDEN = 4
VMEM = pltpu.VMEM


def dot(a, b):
    return jnp.dot(a, b, preferred_element_type=F32)


def contract_last(a, b):
    return lax.dot_general(a, b, (((1,), (1,)), ((), ())), preferred_element_type=F32)


def contract_first(a, b):
    return lax.dot_general(a, b, (((0,), (0,)), ((), ())), preferred_element_type=F32)


def exact_ones(condition):
    return jnp.where(condition, 1.0, 0.0).astype(BF16)


def near(n, size):
    return lax.rem(((n + 1) // 2) * (2 * lax.rem(n, 2) - 1) + size, size)


def kernel(
    tok, cot, krow, kcol, gate_hbm, up_hbm, down_hbm,
    out_tok, out_gate, out_up, out_down,
    wg, wu, wd, wide, place, fetch, perm, perm_t, sent, got, rows_of, back_rows, q_out, q_in, part_out, part_in,
    gate, lift, hid, dgate, dup, q_own, own, acc_gate, acc_up, acc_down, swap_out, swap_in, state, grad,
    sem_w, sem_send, sem_got, sem_xs, sem_xr, sem_hs, sem_hr, sem_qs, sem_qr, sem_ps, sem_pr, sem_ds, sem_dr,
):
    me = lax.axis_index("expert")
    h = lax.axis_index("hidden")
    y, z, core = me // 16, lax.rem(me // 2, 8), lax.rem(me, 2)
    right, left, across = lax.rem(h + 1, HIDDEN), lax.rem(h + 3, HIDDEN), lax.rem(h + 2, HIDDEN)

    loads = [
        pltpu.make_async_copy(gate_hbm, wg, sem_w.at[0]),
        pltpu.make_async_copy(up_hbm, wu, sem_w.at[1]),
    ] + [
        pltpu.make_async_copy(down_hbm.at[:, pl.ds(k * 512, 512)], wd.at[k], sem_w.at[2 + k])
        for k in range(HIDDEN)
    ]
    for load in loads:
        load.start()

    barrier = pltpu.get_barrier_semaphore()

    def greet(j, carry):
        pl.semaphore_signal(barrier, inc=1, device_id=(lax.rem(me + j, EXPERTS), h), device_id_type=MESH)
        return carry

    lax.fori_loop(1, EXPERTS, greet, 0)
    for o in (1, 2, 3):
        pl.semaphore_signal(barrier, inc=1, device_id=(me, lax.rem(h + o, HIDDEN)), device_id_type=MESH)

    def build(visit):
        def step(g, carry):
            rows = pl.ds(pl.multiple_of(g * 256, 256), 256)
            numbers = lax.broadcasted_iota(jnp.int32, (256, 512), 0) + g * 256
            place[visit, rows, :] = exact_ones(numbers == krow[visit])
            half = pl.ds(pl.multiple_of(g * 128, 128), 128)
            across_lanes = lax.broadcasted_iota(jnp.int32, (128, 1024), 1)
            fetch[visit, half, :] = exact_ones(across_lanes == kcol[visit, half, :])
            return carry

        lax.fori_loop(0, 4, step, 0)

    def image(slot_number):
        c, s = slot_number // 64, slot_number % 64
        return (s // 4) * 16 + c * 4 + s % 4

    first = lax.broadcasted_iota(jnp.int32, (256, 256), 0)
    second = lax.broadcasted_iota(jnp.int32, (256, 256), 1)
    perm[...] = exact_ones(second == image(first))
    perm_t[...] = exact_ones(first == image(second))
    build(0)
    state[...] = tok[...]
    grad[...] = cot[...]
    pl.semaphore_wait(barrier, EXPERTS - 1 + HIDDEN - 1)

    pending = []

    def send_group(n, g, forward):
        def go(t, carry):
            i = g * 16 + 15 - t
            dy, dz, dc = near(i // 16, 4), near(lax.rem(i // 2, 8), 8), lax.rem(i, 2)
            if not forward:
                dy, dz = 4 - dy, 8 - dz
            peer = lax.rem(y + dy, 4) * 16 + lax.rem(z + dz, 8) * 2 + lax.rem(core + dc, 2)
            rows = pl.ds(pl.multiple_of(i * 16, 16), 16)
            pltpu.make_async_remote_copy(
                src_ref=sent.at[n, rows], dst_ref=got.at[n, rows],
                send_sem=sem_send.at[n, g // 2], recv_sem=sem_got.at[n, g // 2],
                device_id=(peer, h), device_id_type=MESH,
            ).start()
            return carry

        lax.fori_loop(0, 16 if g else 15, go, 0)

    def exchanged(n, half):
        rows = pl.ds(16, 31 * 16) if half == 0 else pl.ds(32 * 16, 32 * 16)
        copy = pltpu.make_async_remote_copy(
            src_ref=sent.at[n, rows], dst_ref=got.at[n, rows],
            send_sem=sem_send.at[n, half], recv_sem=sem_got.at[n, half],
            device_id=(lax.rem(me + 1, EXPERTS), h), device_id_type=MESH,
        )
        copy.wait_recv()
        pending.append(copy)

    def stacked(values):
        return jnp.concatenate([values[:, c * 128 : (c + 1) * 128] for c in range(4)], axis=0)

    def dispatch(n, visit, values):
        values = stacked(values.astype(BF16))
        for g in range(4):
            rows = pl.ds(g * 256, 256)
            sent[n, rows, :] = dot(place[visit, rows, :], values).astype(BF16)
            send_group(n, g, True)
        got[n, 0:16, :] = sent[n, 0:16, :]

    def return_rows(n, half, total):
        total = total.astype(BF16)
        for g in (2 * half + 1, 2 * half):
            piece = total[(g % 2) * 64 : (g % 2) * 64 + 64]
            sent[n, pl.ds(g * 256, 256), :] = dot(perm_t[...], stacked(piece)).astype(BF16)
            send_group(n, g, False)
        if half == 0:
            got[n, 0:16, :] = sent[n, 0:16, :]

    def arrive(n, visit, target):
        exchanged(n, 1)
        exchanged(n, 0)
        back = dot(fetch[visit], got[n])
        for c in range(4):
            target[:, pl.ds(c * 128, 128)] += back[c * 128 : (c + 1) * 128]

    def hand(ref_from, ref_to, s, r, side):
        copy = pltpu.make_async_remote_copy(
            src_ref=ref_from, dst_ref=ref_to, send_sem=s, recv_sem=r,
            device_id=(me, side), device_id_type=MESH,
        )
        copy.start()
        pending.append(copy)

    def awaited(ref, s, r):
        pltpu.make_async_remote_copy(
            src_ref=ref, dst_ref=ref, send_sem=s, recv_sem=r, device_id=(me, right), device_id_type=MESH
        ).wait_recv()

    def at_offset(o):
        return lax.rem(h + o, HIDDEN)

    def placed_rows(n, target, g):
        turned = dot(perm[...], got[n, pl.ds(g * 256, 256), :]).astype(BF16)
        for c in range(4):
            target[pl.ds(g * 64, 64), pl.ds(c * 128, 128)] = turned[c * 64 : (c + 1) * 64]

    def spread(n, d):
        for g in range(4):
            if g % 2 == 0:
                exchanged(n, g // 2)
            placed_rows(n, rows_of.at[d, h], g)
            mine = rows_of.at[d, h, pl.ds(g * 64, 64)]
            hand(mine, mine, sem_xs.at[d, 0, g], sem_xr.at[d, 0, g], right)
            hand(mine, mine, sem_xs.at[d, 1, g], sem_xr.at[d, 1, g], left)

    def relay(d):
        for g in range(4):
            rows = pl.ds(g * 64, 64)
            from_left, from_right = rows_of.at[d, left, rows], rows_of.at[d, right, rows]
            awaited(from_left, sem_xs.at[d, 0, g], sem_xr.at[d, 0, g])
            if g % 2 == 0:
                hand(from_left, from_left, sem_xs.at[d, 2, g], sem_xr.at[d, 2, g], right)
            awaited(from_right, sem_xs.at[d, 1, g], sem_xr.at[d, 1, g])
            if g % 2 == 1:
                hand(from_right, from_right, sem_xs.at[d, 2, g], sem_xr.at[d, 2, g], left)

    def lift_up(visit):
        def use(k, start):
            a = rows_of[visit, k]
            if start:
                gate[visit] = dot(a, wg[k])
                lift[visit] = dot(a, wu[k])
            else:
                gate[visit] += dot(a, wg[k])
                lift[visit] += dot(a, wu[k])

        use(h, True)
        relay(visit)
        use(left, False)
        use(right, False)
        for g in range(4):
            awaited(rows_of.at[visit, across, pl.ds(g * 64, 64)], sem_xs.at[visit, 2, g], sem_xr.at[visit, 2, g])
        use(across, False)
        value = gate[visit]
        hid[visit, h] = (jax.nn.sigmoid(value) * value * lift[visit]).astype(BF16)

    def share_hidden(visit):
        for half in (1, 0):
            mine = hid.at[visit, h, pl.ds(half * 128, 128)]
            for o in (2, 1, 3):
                hand(mine, mine, sem_hs.at[visit, o - 1, half], sem_hr.at[visit, o - 1, half], at_offset(o))

    def hidden_shared(visit, half):
        for o in (1, 3, 2):
            ref = hid.at[visit, at_offset(4 - o), pl.ds(half * 128, 128)]
            awaited(ref, sem_hs.at[visit, o - 1, half], sem_hr.at[visit, o - 1, half])

    def put_down(n, visit):
        share_hidden(visit)
        for half in (1, 0):
            hidden_shared(visit, half)
            rows = pl.ds(half * 128, 128)
            total = dot(hid[visit, 0, rows, :], wide[0])
            for k in range(1, HIDDEN):
                total += dot(hid[visit, k, rows, :], wide[k])
            return_rows(n, half, total)

    def collect(n, visit):
        for half in range(2):
            exchanged(n, half)
            for g in (2 * half, 2 * half + 1):
                placed_rows(n, back_rows.at[visit], g)
            rows = pl.ds(half * 128, 128)
            b = back_rows[visit, rows, :]
            for o in (2, 1, 3):
                q_out[visit, o - 1, rows, :] = contract_last(b, wide[at_offset(o)]).astype(BF16)
                hand(
                    q_out.at[visit, o - 1, rows], q_in.at[visit, o - 1, rows],
                    sem_qs.at[visit, o - 1, half], sem_qr.at[visit, o - 1, half], at_offset(o),
                )
            q_own[visit, rows, :] = contract_last(b, wide[h])

    def collected(visit):
        for half in range(2):
            rows = pl.ds(half * 128, 128)
            for o in (1, 3, 2):
                awaited(q_in.at[visit, o - 1, rows], sem_qs.at[visit, o - 1, half], sem_qr.at[visit, o - 1, half])
        q_own[visit] += sum(q_in[visit, o].astype(F32) for o in range(3))

    def derive(visit):
        q, value = q_own[visit], gate[visit]
        sigma = jax.nn.sigmoid(value)
        dgate[...] = (q * lift[visit] * sigma * (1.0 + value * (1.0 - sigma))).astype(BF16)
        dup[...] = (q * (value * sigma)).astype(BF16)

    def put_back(n, visit):
        def part(k, rows):
            return contract_last(dgate[rows, :], wg[k]) + contract_last(dup[rows, :], wu[k])

        for half in (1, 0):
            rows = pl.ds(half * 128, 128)
            for o in (2, 1, 3):
                part_out[visit, o - 1, rows, :] = part(at_offset(o), rows).astype(BF16)
                hand(
                    part_out.at[visit, o - 1, rows], part_in.at[visit, o - 1, rows],
                    sem_ps.at[visit, o - 1, half], sem_pr.at[visit, o - 1, half], at_offset(o),
                )
        for half in (1, 0):
            rows = pl.ds(half * 128, 128)
            own[rows, :] = part(h, rows)
        for half in (1, 0):
            rows = pl.ds(half * 128, 128)
            for o in (1, 3, 2):
                awaited(part_in.at[visit, o - 1, rows], sem_ps.at[visit, o - 1, half], sem_pr.at[visit, o - 1, half])
            total = own[rows, :] + sum(part_in[visit, o, rows, :].astype(F32) for o in range(3))
            return_rows(n, half, total)

    def weigh(visit):
        def step(k, carry):
            a = rows_of[visit, k]
            by_gate = contract_first(a, dgate[...])
            by_up = contract_first(a, dup[...])
            if visit < 2:
                by_gate += acc_gate[k]
                by_up += acc_up[k]
            if visit > 0:
                acc_gate[k] = by_gate
                acc_up[k] = by_up
            else:
                rows = pl.ds(pl.multiple_of(k * 512, 512), 512)
                out_gate[rows, :] = by_gate.astype(BF16)
                out_up[rows, :] = by_up.astype(BF16)
            return carry

        lax.fori_loop(0, HIDDEN, step, 0)

    def weigh_down(visit):
        def step(k, carry):
            by_down = contract_first(hid[visit, k], back_rows[visit])
            if visit < 2:
                by_down += acc_down[k]
            if visit > 0:
                acc_down[k] = by_down
            else:
                swap_out[k] = by_down.astype(BF16)
            return carry

        lax.fori_loop(0, HIDDEN, step, 0)

    dispatch(0, 0, state[...])
    for load in loads:
        load.wait()
    for o in (2, 1, 3):
        hand(wd.at[at_offset(o)], wide.at[h], sem_ds.at[0, o - 1], sem_dr.at[0, o - 1], at_offset(o))
    wide[h] = wd[h]
    build(2)
    spread(0, 0)
    dispatch(1, 2, grad[...])
    lift_up(0)
    for o in (1, 2, 3):
        awaited(wide.at[at_offset(4 - o)], sem_ds.at[0, o - 1], sem_dr.at[0, o - 1])
    put_down(2, 0)
    build(1)
    collect(1, 2)
    arrive(2, 0, state)

    dispatch(3, 1, state[...])
    collected(2)
    spread(3, 1)
    lift_up(1)
    put_down(4, 1)
    arrive(4, 1, state)

    dispatch(5, 2, state[...])
    spread(5, 2)
    lift_up(2)
    derive(2)
    put_back(6, 2)
    share_hidden(2)
    weigh(2)
    arrive(6, 2, grad)

    dispatch(7, 1, grad[...])
    collect(7, 1)
    collected(1)
    derive(1)
    put_back(8, 1)
    for half in range(2):
        hidden_shared(2, half)
    weigh(1)
    weigh_down(2)
    weigh_down(1)
    arrive(8, 1, grad)

    dispatch(9, 0, grad[...])
    collect(9, 0)
    weigh_down(0)
    collected(0)
    derive(0)
    put_back(10, 0)
    for o in (2, 1, 3):
        hand(swap_out.at[at_offset(o)], swap_in.at[h], sem_ds.at[1, o - 1], sem_dr.at[1, o - 1], at_offset(o))
    swap_in[h] = swap_out[h]
    weigh(0)
    arrive(10, 0, grad)
    out_tok[...] = grad[...]
    for o in (1, 2, 3):
        awaited(swap_in.at[at_offset(4 - o)], sem_ds.at[1, o - 1], sem_dr.at[1, o - 1])
    for k in range(HIDDEN):
        out_down[:, pl.ds(k * 512, 512)] = swap_in[k]
    for copy in pending:
        copy.wait_send()


def body(
    tokens, route_first, route_second, route_third, gate_weight, up_weight, down_weight, cotangent
):
    count, width = tokens.shape
    me = lax.axis_index("expert")
    owner = jnp.stack([route[:, 0] for route in (route_first, route_second, route_third)])
    earlier = jnp.arange(count)[None, :] < jnp.arange(count)[:, None]
    same = (owner[:, :, None] == owner[:, None, :]) & earlier[None]
    rank = jnp.sum(same.astype(jnp.int32), axis=2)

    def nearness(there, here, size):
        gap = lax.rem(there - here + size, size)
        return jnp.where(gap == 0, 0, jnp.where(gap <= size // 2, 2 * gap - 1, 2 * (size - gap)))

    position = (
        nearness(owner // 16, me // 16, 4) * 16
        + nearness(lax.rem(owner // 2, 8), lax.rem(me // 2, 8), 8) * 2
        + lax.rem(owner + me, 2)
    )
    base = position * (4 * RANKS) + rank
    keys = base[:, None, :] + RANKS * jnp.arange(4, dtype=jnp.int32)[None, :, None]
    keys = keys.reshape(3, 4 * count)

    in_vmem = pl.BlockSpec(memory_space=VMEM)
    anywhere = pl.BlockSpec(memory_space=pl.ANY)
    dma = pltpu.SemaphoreType.DMA
    results = pl.pallas_call(
        kernel,
        out_shape=(
            jax.ShapeDtypeStruct((count, width), F32),
            jax.ShapeDtypeStruct((2048, 256), BF16),
            jax.ShapeDtypeStruct((2048, 256), BF16),
            jax.ShapeDtypeStruct((256, 2048), BF16),
        ),
        in_specs=[in_vmem] * 4 + [anywhere] * 3,
        out_specs=(in_vmem,) * 4,
        scratch_shapes=[
            VMEM((4, 512, 256), BF16),
            VMEM((4, 512, 256), BF16),
            VMEM((4, 256, 512), BF16),
            VMEM((4, 256, 512), BF16),
            VMEM((3, 1024, 512), BF16),
            VMEM((3, 512, 1024), BF16),
            VMEM((256, 256), BF16),
            VMEM((256, 256), BF16),
            VMEM((11, 1024, 128), BF16),
            VMEM((11, 1024, 128), BF16),
            VMEM((3, 4, 256, 512), BF16),
            VMEM((3, 256, 512), BF16),
            VMEM((3, 3, 256, 256), BF16),
            VMEM((3, 3, 256, 256), BF16),
            VMEM((3, 3, 256, 512), BF16),
            VMEM((3, 3, 256, 512), BF16),
            VMEM((3, 256, 256), F32),
            VMEM((3, 256, 256), F32),
            VMEM((3, 4, 256, 256), BF16),
            VMEM((256, 256), BF16),
            VMEM((256, 256), BF16),
            VMEM((3, 256, 256), F32),
            VMEM((256, 512), F32),
            VMEM((4, 512, 256), F32),
            VMEM((4, 512, 256), F32),
            VMEM((4, 256, 512), F32),
            VMEM((4, 256, 512), BF16),
            VMEM((4, 256, 512), BF16),
            VMEM((128, 512), F32),
            VMEM((128, 512), F32),
            dma((6,)),
            dma((11, 2)),
            dma((11, 2)),
            dma((3, 3, 4)),
            dma((3, 3, 4)),
            dma((3, 3, 2)),
            dma((3, 3, 2)),
            dma((3, 3, 2)),
            dma((3, 3, 2)),
            dma((3, 3, 2)),
            dma((3, 3, 2)),
            dma((2, 3)),
            dma((2, 3)),
        ],
        compiler_params=pltpu.CompilerParams(
            collective_id=0, has_side_effects=True, vmem_limit_bytes=48 * 2**20
        ),
    )(
        tokens,
        cotangent,
        keys[:, None, :],
        keys[:, :, None],
        gate_weight.reshape(4, 512, 256),
        up_weight.reshape(4, 512, 256),
        down_weight[0],
    )
    a, b, c, d = results
    return a, b[None], c[None], d[None]


def solution(mesh):
    placed = (
        P("expert", "hidden"),
        P("expert", None),
        P("expert", None),
        P("expert", None),
        P("expert", None, "hidden"),
        P("expert", None, "hidden"),
        P("expert", "hidden", None),
        P("expert", "hidden"),
    )
    return jax.shard_map(
        body,
        mesh=mesh,
        in_specs=placed,
        out_specs=(
            P("expert", "hidden"),
            P("expert", None, "hidden"),
            P("expert", None, "hidden"),
            P("expert", "hidden", None),
        ),
        check_vma=False,
    )
```

time: 235 us -> 218 us (0.928)
  Pallas kernels: 224 us -> 211 us
    pallas_call x1, Pallas kernels: 224 us -> 211 us  [body(): pl.pallas_call(kernel, out_shape=(jax.ShapeDtypeStruct((count, width), F3...]
    unnamed x14 -> x16, local copies, waits for them, and re-layouts: 7.19 us -> 5.16 us
where the time goes in v2:
time: 218 us
  Pallas kernels  211 us (97%)
  local copies, waits for them, and re-layouts  5.86 us (3%)
    pallas_call x1, Pallas kernels, body(): pl.pallas_call(kernel, out_shape=(jax.ShapeDtypeStruct((count, width), F3...  211 us
    unnamed x16, local copies, waits for them, and re-layouts  5.16 us

profile of v2, /device:TPU:1, one launch (start us, length us, event | category | flops | bytes accessed | tf_op | source)
XLA Modules:
  0.0 217.7 jit_solution(10182049222191062233)
XLA Ops:
  0.7 0.0 copy-start.3
  0.7 0.0 copy-start.4
  0.7 0.0 copy-start.5
  0.7 0.1 broadcast_bitcast_fusion
  0.8 0.6 copy-done.3
  1.3 0.0 copy-done.4
  1.3 0.0 copy-done.5
  1.4 0.2 convert_reduce_fusion
  1.7 0.0 copy-start
  1.7 0.6 add.126
  2.3 0.0 copy-start.1
  2.3 0.0 copy-start.2
  2.4 0.1 broadcast_add_fusion.kcol
  2.5 0.4 copy-done
  2.9 0.4 copy-done.1
  3.4 0.1 copy-done.2
  3.4 210.6 %shard_map.111 = (f32[128,512]{1,0:T(8,128)S(1)}, bf16[2048,256]{1,0:T(8,128)(2,1)S(1)}, bf16[2048,256]{1,0:T(8,128)(2,1)S(1)}, bf16[256,2048]{1,0:T(8,128)(2,1)S(1)}) custom-call(f32[128,512]{1,0:T(8,128)S(1)} %copy-done.1, f32[128,512]{1,0:T(8,128)S(1)} %copy-done.2, s32[3,1,512]{2,1,0:T(1,128)S(1)} %broadcast_add_fusion.1.krow, ...), custom_call_target="tpu_custom_call" | custom-call | tf_op jit(solution)/shard_map/pallas_call | solution.py:405
  214.0 0.7 copy.20
  214.7 1.0 copy.21
  215.7 1.0 copy.22
  216.7 1.0 copy.23
  (6 shorter events, 0.1 us)
Async XLA Ops:
  0.7 0.7 copy-start.3
  0.7 0.7 copy-start.4
  0.7 0.7 copy-start.5
  1.7 1.2 copy-start
  2.3 1.0 copy-start.1
  2.3 1.1 copy-start.2

commit v3 on v2

--- a/solution.py
+++ b/solution.py
@@ -37,7 +37,7 @@
 def kernel(
     tok, cot, krow, kcol, gate_hbm, up_hbm, down_hbm,
     out_tok, out_gate, out_up, out_down,
-    wg, wu, wd, wide, place, fetch, perm, perm_t, sent, got, rows_of, back_rows, q_out, q_in, part_out, part_in,
+    wg, wu, wd, wide, place, fetch, perm, perm_t, sent, got, rows_of, back_rows, q_out, q_relayed, q_summed, part_out, relayed, summed,
     gate, lift, hid, dgate, dup, q_own, own, acc_gate, acc_up, acc_down, swap_out, swap_in, state, grad,
     sem_w, sem_send, sem_got, sem_xs, sem_xr, sem_hs, sem_hr, sem_qs, sem_qr, sem_ps, sem_pr, sem_ds, sem_dr,
 ):
@@ -142,8 +142,9 @@
 
     def arrive(n, visit, target):
         exchanged(n, 1)
+        back = dot(fetch[visit, :, 512:1024], got[n, 512:1024, :])
         exchanged(n, 0)
-        back = dot(fetch[visit], got[n])
+        back += dot(fetch[visit, :, 0:512], got[n, 0:512, :])
         for c in range(4):
             target[:, pl.ds(c * 128, 128)] += back[c * 128 : (c + 1) * 128]
 
@@ -188,6 +189,15 @@
             if g % 2 == 1:
                 hand(from_right, from_right, sem_xs.at[d, 2, g], sem_xr.at[d, 2, g], left)
 
+    def in_order(d, use):
+        use(h, True)
+        relay(d)
+        use(left, False)
+        use(right, False)
+        for g in range(4):
+            awaited(rows_of.at[d, across, pl.ds(g * 64, 64)], sem_xs.at[d, 2, g], sem_xr.at[d, 2, g])
+        use(across, False)
+
     def lift_up(visit):
         def use(k, start):
             a = rows_of[visit, k]
@@ -198,13 +208,7 @@
                 gate[visit] += dot(a, wg[k])
                 lift[visit] += dot(a, wu[k])
 
-        use(h, True)
-        relay(visit)
-        use(left, False)
-        use(right, False)
-        for g in range(4):
-            awaited(rows_of.at[visit, across, pl.ds(g * 64, 64)], sem_xs.at[visit, 2, g], sem_xr.at[visit, 2, g])
-        use(across, False)
+        in_order(visit, use)
         value = gate[visit]
         hid[visit, h] = (jax.nn.sigmoid(value) * value * lift[visit]).astype(BF16)
 
@@ -229,27 +233,63 @@
                 total += dot(hid[visit, k, rows, :], wide[k])
             return_rows(n, half, total)
 
+    def over_hidden(order, ready, part, out, passing, arriving, mine, s, r):
+        rows = [pl.ds(0, 128), pl.ds(128, 128)]
+        for half in order:
+            side, other, slot = ((right, left, 2), (left, right, 1))[half]
+            ready(half)
+            out[0, rows[half], :] = part(across, half).astype(BF16)
+            hand(out.at[0, rows[half]], passing.at[half], s.at[half], r.at[half], side)
+            out[slot, rows[half], :] = part(other, half).astype(BF16)
+            hand(out.at[slot, rows[half]], arriving.at[slot - 1, rows[half]], s.at[2 + half], r.at[2 + half], other)
+        for half in order:
+            side, slot = ((right, 1), (left, 2))[half]
+            value = part(side, half)
+            awaited(passing.at[half], s.at[half], r.at[half])
+            out[slot, rows[half], :] = (value + passing[half].astype(F32)).astype(BF16)
+            hand(out.at[slot, rows[half]], arriving.at[slot - 1, rows[half]], s.at[4 + half], r.at[4 + half], side)
+        for half in order:
+            mine[rows[half], :] = part(h, half)
+
+    def over_hidden_done(arriving, mine, s, r, half):
+        rows = pl.ds(half * 128, 128)
+        from_left, from_right = (4, 2) if half == 0 else (3, 5)
+        awaited(arriving.at[0, rows], s.at[from_left], r.at[from_left])
+        awaited(arriving.at[1, rows], s.at[from_right], r.at[from_right])
+        return mine[rows, :] + arriving[0, rows, :].astype(F32) + arriving[1, rows, :].astype(F32)
+
     def collect(n, visit):
-        for half in range(2):
+        d = visit - 1
+
+        def ready(half):
             exchanged(n, half)
             for g in (2 * half, 2 * half + 1):
-                placed_rows(n, back_rows.at[visit], g)
-            rows = pl.ds(half * 128, 128)
-            b = back_rows[visit, rows, :]
-            for o in (2, 1, 3):
-                q_out[visit, o - 1, rows, :] = contract_last(b, wide[at_offset(o)]).astype(BF16)
-                hand(
-                    q_out.at[visit, o - 1, rows], q_in.at[visit, o - 1, rows],
-                    sem_qs.at[visit, o - 1, half], sem_qr.at[visit, o - 1, half], at_offset(o),
-                )
-            q_own[visit, rows, :] = contract_last(b, wide[h])
+                placed_rows(n, back_rows.at[d], g)
+
+        def part(k, half):
+            return contract_last(back_rows[d, pl.ds(half * 128, 128), :], wide[k])
+
+        over_hidden(
+            (0, 1), ready, part, q_out.at[d], q_relayed.at[d], q_summed.at[d], q_own.at[visit], sem_qs.at[d], sem_qr.at[d]
+        )
 
     def collected(visit):
+        d = visit - 1
         for half in range(2):
-            rows = pl.ds(half * 128, 128)
-            for o in (1, 3, 2):
-                awaited(q_in.at[visit, o - 1, rows], sem_qs.at[visit, o - 1, half], sem_qr.at[visit, o - 1, half])
-        q_own[visit] += sum(q_in[visit, o].astype(F32) for o in range(3))
+            total = over_hidden_done(q_summed.at[d], q_own.at[visit], sem_qs.at[d], sem_qr.at[d], half)
+            q_own[visit, pl.ds(half * 128, 128), :] = total
+
+    def collect_whole(n, d):
+        spread(n, d)
+
+        def use(k, start):
+            value = contract_last(rows_of[d, k], wd[k])
+            if start:
+                q_own[0] = value
+            else:
+                q_own[0] += value
+
+        in_order(d, use)
 
     def derive(visit):
         q, value = q_own[visit], gate[visit]
@@ -258,25 +298,16 @@
         dup[...] = (q * (value * sigma)).astype(BF16)
 
     def put_back(n, visit):
-        def part(k, rows):
+        def part(k, half):
+            rows = pl.ds(half * 128, 128)
             return contract_last(dgate[rows, :], wg[k]) + contract_last(dup[rows, :], wu[k])
 
+        over_hidden(
+            (1, 0), lambda half: None, part, part_out.at[visit], relayed.at[visit], summed.at[visit], own,
+            sem_ps.at[visit], sem_pr.at[visit],
+        )
         for half in (1, 0):
-            rows = pl.ds(half * 128, 128)
-            for o in (2, 1, 3):
-                part_out[visit, o - 1, rows, :] = part(at_offset(o), rows).astype(BF16)
-                hand(
-                    part_out.at[visit, o - 1, rows], part_in.at[visit, o - 1, rows],
-                    sem_ps.at[visit, o - 1, half], sem_pr.at[visit, o - 1, half], at_offset(o),
-                )
-        for half in (1, 0):
-            rows = pl.ds(half * 128, 128)
-            own[rows, :] = part(h, rows)
-        for half in (1, 0):
-            rows = pl.ds(half * 128, 128)
-            for o in (1, 3, 2):
-                awaited(part_in.at[visit, o - 1, rows], sem_ps.at[visit, o - 1, half], sem_pr.at[visit, o - 1, half])
-            total = own[rows, :] + sum(part_in[visit, o, rows, :].astype(F32) for o in range(3))
+            total = over_hidden_done(summed.at[visit], own, sem_ps.at[visit], sem_pr.at[visit], half)
             return_rows(n, half, total)
 
     def weigh(visit):
@@ -300,13 +331,11 @@
 
     def weigh_down(visit):
         def step(k, carry):
-            by_down = contract_first(hid[visit, k], back_rows[visit])
+            by_down = contract_first(hid[visit, k], back_rows[visit - 1])
             if visit < 2:
-                by_down += acc_down[k]
-            if visit > 0:
+                swap_out[k] = (by_down + acc_down[k]).astype(BF16)
+            else:
                 acc_down[k] = by_down
-            else:
-                swap_out[k] = by_down.astype(BF16)
             return carry
 
         lax.fori_loop(0, HIDDEN, step, 0)
@@ -354,24 +383,23 @@
     weigh(1)
     weigh_down(2)
     weigh_down(1)
-    arrive(8, 1, grad)
-
-    dispatch(9, 0, grad[...])
-    collect(9, 0)
-    weigh_down(0)
-    collected(0)
-    derive(0)
-    put_back(10, 0)
     for o in (2, 1, 3):
         hand(swap_out.at[at_offset(o)], swap_in.at[h], sem_ds.at[1, o - 1], sem_dr.at[1, o - 1], at_offset(o))
     swap_in[h] = swap_out[h]
+    arrive(8, 1, grad)
+
+    dispatch(9, 0, grad[...])
+    collect_whole(9, 3)
+    derive(0)
+    put_back(10, 0)
     weigh(0)
-    arrive(10, 0, grad)
-    out_tok[...] = grad[...]
     for o in (1, 2, 3):
         awaited(swap_in.at[at_offset(4 - o)], sem_ds.at[1, o - 1], sem_dr.at[1, o - 1])
     for k in range(HIDDEN):
-        out_down[:, pl.ds(k * 512, 512)] = swap_in[k]
+        by_down = contract_first(hid[0, h], rows_of[3, k]) + swap_in[k].astype(F32)
+        out_down[:, pl.ds(k * 512, 512)] = by_down.astype(BF16)
+    arrive(10, 0, grad)
+    out_tok[...] = grad[...]
     for copy in pending:
         copy.wait_send()
 
@@ -423,12 +451,14 @@
             VMEM((256, 256), BF16),
             VMEM((11, 1024, 128), BF16),
             VMEM((11, 1024, 128), BF16),
-            VMEM((3, 4, 256, 512), BF16),
-            VMEM((3, 256, 512), BF16),
-            VMEM((3, 3, 256, 256), BF16),
-            VMEM((3, 3, 256, 256), BF16),
+            VMEM((4, 4, 256, 512), BF16),
+            VMEM((2, 256, 512), BF16),
+            VMEM((2, 3, 256, 256), BF16),
+            VMEM((2, 2, 128, 256), BF16),
+            VMEM((2, 2, 256, 256), BF16),
             VMEM((3, 3, 256, 512), BF16),
-            VMEM((3, 3, 256, 512), BF16),
+            VMEM((3, 2, 128, 512), BF16),
+            VMEM((3, 2, 256, 512), BF16),
             VMEM((3, 256, 256), F32),
             VMEM((3, 256, 256), F32),
             VMEM((3, 4, 256, 256), BF16),
@@ -446,14 +476,14 @@
             dma((6,)),
             dma((11, 2)),
             dma((11, 2)),
-            dma((3, 3, 4)),
-            dma((3, 3, 4)),
+            dma((4, 3, 4)),
+            dma((4, 3, 4)),
             dma((3, 3, 2)),
             dma((3, 3, 2)),
-            dma((3, 3, 2)),
-            dma((3, 3, 2)),
-            dma((3, 3, 2)),
-            dma((3, 3, 2)),
+            dma((2, 6)),
+            dma((2, 6)),
+            dma((3, 6)),
+            dma((3, 6)),
             dma((2, 3)),
             dma((2, 3)),
         ],

time: 218 us -> 214 us (0.982)
  Pallas kernels: 211 us -> 206 us
    pallas_call x1, Pallas kernels: 211 us -> 206 us  [body(): pl.pallas_call(kernel, out_shape=(jax.ShapeDtypeStruct((count, width), F3...]
where the time goes in v3:
time: 214 us
  Pallas kernels  206 us (96%)
  local copies, waits for them, and re-layouts  5.86 us (3%)
    pallas_call x1, Pallas kernels, body(): pl.pallas_call(kernel, out_shape=(jax.ShapeDtypeStruct((count, width), F3...  206 us
    unnamed x16, local copies, waits for them, and re-layouts  5.16 us

profile of v3, /device:TPU:1, one launch (start us, length us, event | category | flops | bytes accessed | tf_op | source)
XLA Modules:
  0.0 213.5 jit_solution(18261583057614785226)
XLA Ops:
  0.7 0.0 copy-start.3
  0.7 0.0 copy-start.4
  0.7 0.0 copy-start.5
  0.7 0.1 broadcast_bitcast_fusion
  0.8 0.6 copy-done.3
  1.3 0.0 copy-done.4
  1.3 0.0 copy-done.5
  1.4 0.2 convert_reduce_fusion
  1.7 0.0 copy-start
  1.7 0.6 add.126
  2.3 0.0 copy-start.1
  2.3 0.0 copy-start.2
  2.4 0.1 broadcast_add_fusion.kcol
  2.5 0.4 copy-done
  2.9 0.4 copy-done.1
  3.4 0.1 copy-done.2
  3.4 206.4 %shard_map.111 = (f32[128,512]{1,0:T(8,128)S(1)}, bf16[2048,256]{1,0:T(8,128)(2,1)S(1)}, bf16[2048,256]{1,0:T(8,128)(2,1)S(1)}, bf16[256,2048]{1,0:T(8,128)(2,1)S(1)}) custom-call(f32[128,512]{1,0:T(8,128)S(1)} %copy-done.1, f32[128,512]{1,0:T(8,128)S(1)} %copy-done.2, s32[3,1,512]{2,1,0:T(1,128)S(1)} %broadcast_add_fusion.1.krow, ...), custom_call_target="tpu_custom_call" | custom-call | tf_op jit(solution)/shard_map/pallas_call | solution.py:433
  209.9 0.7 copy.20
  210.6 1.0 copy.21
  211.6 1.0 copy.22
  212.5 1.0 copy.23
  (6 shorter events, 0.1 us)
Async XLA Ops:
  0.7 0.7 copy-start.3
  0.7 0.7 copy-start.4
  0.7 0.7 copy-start.5
  1.7 1.2 copy-start
  2.3 1.0 copy-start.1
  2.3 1.1 copy-start.2

commit v4 on v3

--- a/solution.py
+++ b/solution.py
@@ -35,9 +35,9 @@
 
 
 def kernel(
-    tok, cot, krow, kcol, gate_hbm, up_hbm, down_hbm,
+    tok, cot, route_0, route_1, route_2, gate_hbm, up_hbm, down_hbm,
     out_tok, out_gate, out_up, out_down,
-    wg, wu, wd, wide, place, fetch, perm, perm_t, sent, got, rows_of, back_rows, q_out, q_relayed, q_summed, part_out, relayed, summed,
+    krow, kcol, wg, wu, wd, wide, place, fetch, perm, perm_t, sent, got, rows_of, back_rows, q_out, q_relayed, q_summed, part_out, relayed, summed,
     gate, lift, hid, dgate, dup, q_own, own, acc_gate, acc_up, acc_down, swap_out, swap_in, state, grad,
     sem_w, sem_send, sem_got, sem_xs, sem_xr, sem_hs, sem_hr, sem_qs, sem_qr, sem_ps, sem_pr, sem_ds, sem_dr,
 ):
@@ -55,6 +55,12 @@
     ]
     for load in loads:
         load.start()
+    starts = [
+        pltpu.make_async_copy(tok, state, sem_w.at[6]),
+        pltpu.make_async_copy(cot, grad, sem_w.at[7]),
+    ]
+    for start in starts:
+        start.start()
 
     barrier = pltpu.get_barrier_semaphore()
 
@@ -66,7 +72,29 @@
     for o in (1, 2, 3):
         pl.semaphore_signal(barrier, inc=1, device_id=(me, lax.rem(h + o, HIDDEN)), device_id_type=MESH)
 
+    def nearness(gap, size):
+        return jnp.where(gap == 0, 0, jnp.where(gap <= size // 2, 2 * gap - 1, 2 * (size - gap)))
+
+    def keys_of(owner, rank):
+        gap_y = jnp.bitwise_and(jnp.right_shift(owner, 4) - y + 4, 3)
+        gap_z = jnp.bitwise_and(jnp.right_shift(owner, 1) - z + 8, 7)
+        gap_core = jnp.bitwise_and(owner + core, 1)
+        return (nearness(gap_y, 4) * 16 + nearness(gap_z, 8) * 2 + gap_core) * (4 * RANKS) + rank
+
     def build(visit):
+        along = jnp.broadcast_to((route_0, route_1, route_2)[visit][...].astype(F32), (128, 128))
+        down = jnp.transpose(along)
+        token = lax.broadcasted_iota(jnp.int32, (128, 128), 0)
+        other = lax.broadcasted_iota(jnp.int32, (128, 128), 1)
+        same = along == down
+        rank_down = jnp.sum(jnp.where(same & (other < token), 1.0, 0.0), axis=1, keepdims=True)
+        rank_along = jnp.sum(jnp.where(same & (token < other), 1.0, 0.0), axis=0, keepdims=True)
+        key_along = keys_of(along[0:1, :].astype(jnp.int32), rank_along.astype(jnp.int32))
+        key_down = keys_of(down[:, 0:1].astype(jnp.int32), rank_down.astype(jnp.int32))
+        for c in range(4):
+            krow[visit, :, pl.ds(c * 128, 128)] = key_along + RANKS * c
+            kcol[visit, pl.ds(c * 128, 128), :] = key_down + RANKS * c
+
         def step(g, carry):
             rows = pl.ds(pl.multiple_of(g * 256, 256), 256)
             numbers = lax.broadcasted_iota(jnp.int32, (256, 512), 0) + g * 256
@@ -87,8 +115,6 @@
     perm[...] = exact_ones(second == image(first))
     perm_t[...] = exact_ones(first == image(second))
     build(0)
-    state[...] = tok[...]
-    grad[...] = cot[...]
     pl.semaphore_wait(barrier, EXPERTS - 1 + HIDDEN - 1)
 
     pending = []
@@ -340,11 +366,11 @@
 
         lax.fori_loop(0, HIDDEN, step, 0)
 
-    dispatch(0, 0, state[...])
-    for load in loads:
+    for load in loads + starts:
         load.wait()
     for o in (2, 1, 3):
         hand(wd.at[at_offset(o)], wide.at[h], sem_ds.at[0, o - 1], sem_dr.at[0, o - 1], at_offset(o))
+    dispatch(0, 0, state[...])
     wide[h] = wd[h]
     build(2)
     spread(0, 0)
@@ -408,27 +434,8 @@
     tokens, route_first, route_second, route_third, gate_weight, up_weight, down_weight, cotangent
 ):
     count, width = tokens.shape
-    me = lax.axis_index("expert")
-    owner = jnp.stack([route[:, 0] for route in (route_first, route_second, route_third)])
-    earlier = jnp.arange(count)[None, :] < jnp.arange(count)[:, None]
-    same = (owner[:, :, None] == owner[:, None, :]) & earlier[None]
-    rank = jnp.sum(same.astype(jnp.int32), axis=2)
-
-    def nearness(there, here, size):
-        gap = lax.rem(there - here + size, size)
-        return jnp.where(gap == 0, 0, jnp.where(gap <= size // 2, 2 * gap - 1, 2 * (size - gap)))
-
-    position = (
-        nearness(owner // 16, me // 16, 4) * 16
-        + nearness(lax.rem(owner // 2, 8), lax.rem(me // 2, 8), 8) * 2
-        + lax.rem(owner + me, 2)
-    )
-    base = position * (4 * RANKS) + rank
-    keys = base[:, None, :] + RANKS * jnp.arange(4, dtype=jnp.int32)[None, :, None]
-    keys = keys.reshape(3, 4 * count)
-
     in_vmem = pl.BlockSpec(memory_space=VMEM)
-    anywhere = pl.BlockSpec(memory_space=pl.ANY)
+    in_hbm = pl.BlockSpec(memory_space=pltpu.HBM)
     dma = pltpu.SemaphoreType.DMA
     results = pl.pallas_call(
         kernel,
@@ -438,9 +445,11 @@
             jax.ShapeDtypeStruct((2048, 256), BF16),
             jax.ShapeDtypeStruct((256, 2048), BF16),
         ),
-        in_specs=[in_vmem] * 4 + [anywhere] * 3,
+        in_specs=[in_hbm] * 2 + [in_vmem] * 3 + [in_hbm] * 3,
         out_specs=(in_vmem,) * 4,
         scratch_shapes=[
+            VMEM((3, 1, 512), jnp.int32),
+            VMEM((3, 512, 1), jnp.int32),
             VMEM((4, 512, 256), BF16),
             VMEM((4, 512, 256), BF16),
             VMEM((4, 256, 512), BF16),
@@ -473,7 +482,7 @@
             VMEM((4, 256, 512), BF16),
             VMEM((128, 512), F32),
             VMEM((128, 512), F32),
-            dma((6,)),
+            dma((8,)),
             dma((11, 2)),
             dma((11, 2)),
             dma((4, 3, 4)),
@@ -488,13 +497,14 @@
             dma((2, 3)),
         ],
         compiler_params=pltpu.CompilerParams(
-            collective_id=0, has_side_effects=True, vmem_limit_bytes=48 * 2**20
+            collective_id=0, has_side_effects=True, vmem_limit_bytes=54 * 2**20
         ),
     )(
         tokens,
         cotangent,
-        keys[:, None, :],
-        keys[:, :, None],
+        route_first.reshape(1, count),
+        route_second.reshape(1, count),
+        route_third.reshape(1, count),
         gate_weight.reshape(4, 512, 256),
         up_weight.reshape(4, 512, 256),
         down_weight[0],

time: 214 us -> 212 us (level)
    pallas_call x1, Pallas kernels: 206 us -> 204 us  [body(): pl.pallas_call(kernel, out_shape=(jax.ShapeDtypeStruct((count, width), F3...]
    unnamed x16 -> x8, local copies, waits for them, and re-layouts: 5.16 us -> 6.6 us
where the time goes in v4:
time: 212 us; the launch traced here: 211 us
  Pallas kernels  204 us (96%)
  local copies, waits for them, and re-layouts  6.6 us (3%)
    pallas_call x1, Pallas kernels, body(): pl.pallas_call(kernel, out_shape=(jax.ShapeDtypeStruct((count, width), F3...  204 us
    unnamed x8, local copies, waits for them, and re-layouts  6.6 us

profile of v4, /device:TPU:1, one launch (start us, length us, event | category | flops | bytes accessed | tf_op | source)
XLA Modules:
  0.0 211.4 jit_solution(6463244289213854214)
XLA Ops:
  0.6 204.2 %shard_map.111 = (f32[128,512]{1,0:T(8,128)}, bf16[2048,256]{1,0:T(8,128)(2,1)}, bf16[2048,256]{1,0:T(8,128)(2,1)}, bf16[256,2048]{1,0:T(8,128)(2,1)}) custom-call(f32[128,512]{1,0:T(8,128)} %tok.1, f32[128,512]{1,0:T(8,128)} %cot.1, s32[1,128]{1,0:T(1,128)} %bitcast.15, s32[1,128]{1,0:T(1,128)} %bitcast.16, s32[1,128]{1,0:T(1,128)} %bitcast.17, ...), custom_call_target="tpu_custom_call" | custom-call | tf_op jit(solution)/shard_map/pallas_call | solution.py:440
  204.8 1.7 copy.16
  206.5 0.0 copy-start.1
  206.5 2.4 %copy.17 = bf16[1,2048,256]{2,1,0:T(8,128)(2,1)} copy(bf16[1,2048,256]{2,1,0:T(8,128)(2,1)} %bitcast.14) | data formatting | bytes 2097152
  208.8 0.0 copy-done.1
  208.8 0.0 copy-start
  208.8 1.0 copy.18
  209.8 0.6 copy-done
  210.4 1.0 copy.19
Async XLA Ops:
  206.5 2.4 %copy-start.1 = (bf16[2048,256]{1,0:T(8,128)(2,1)S(1)}, bf16[2048,256]{1,0:T(8,128)(2,1)}, u32[]{:S(2)}) copy-start(bf16[2048,256]{1,0:T(8,128)(2,1)} %get-tuple-element.10) | copy-start | bytes 3145732
  208.8 1.6 copy-start
